TPU v7x, 32 devices: a whole 2x2x4 slice. The times are simulated.
32 devices in a mesh: dp: 8 (over y, x, core), mp: 4 (over z).
Axes of the slice: x: 2, y: 2, z: 4, core: 2. Of those that a mesh axis runs over, the one named last changes fastest.
Arguments:
- tokens: bfloat16 [8192, 6144], P('dp', 'mp'), may hold values from -6 to 6
- dest_pos: int32 [8192], P('dp'), may hold values from 0 to 8191, as said below
- src_row: int32 [8192], P('dp'), may hold values from 0 to 8191, as said below
- segment_ids: int32 [8192], P('dp'), may hold values from 0 to 7, as said below
- norm_gain: float32 [6144], replicated, may hold values from 0.1 to 1.9
- qkv_weight: bfloat16 [3, 6144, 3072], P(None, None, 'mp'), may hold values from -0.078125 to 0.078125
- qk_gain: float32 [2, 24, 128], P(None, 'mp'), may hold values from 0.5 to 12
- out_weight: bfloat16 [3072, 6144], P('mp'), may hold values from -0.109375 to 0.109375
Outputs:
- updated: bfloat16 [8192, 6144], P('dp', 'mp')
Inputs may be any that keep to these rules, and one draw needn't show every extreme that they name: `dest_pos`: each index of dp holds 1024 image rows and sends one contiguous block of whole patch rows (16 rows each) to every sequence, the rows keeping their order there; the block sizes of one index of dp are the same numbers for every index, in another order, the largest exactly 192; every sequence receives one block of each size, in a drawn order; each position is named once. `src_row`: the inverse of dest_pos. `segment_ids`: the index of the received block that a position lies in, counted within its sequence; never falling along a sequence.
All inputs are finite; a program needn't handle non-finite values.
Results may differ from a plain program's by a relative error of at most 0.012.
The roundings to bfloat16 on the way count: a program that leaves them out, or rounds other values in their place, can miss the bound.
Values may be sent and summed in bfloat16 or wider, within the bound.
No kernel may reach another device: no remote copies, remote signals or barrier semaphores. Data moves between devices by JAX's collectives and lax.ppermute only.
A program may use at most 192 MiB of HBM per device.

v0:
```python
import math

import jax
import jax.numpy as jnp
from jax import lax
from jax.sharding import PartitionSpec as P

D = 6144
HEAD_DIM = 128


EPS = 1e-06
NEG = -1e30


def norm_rows(values, gain):
    average = jnp.mean(values, axis=-1, keepdims=True)
    centred = values - average
    variance = jnp.mean(centred * centred, axis=-1, keepdims=True)
    return centred * lax.rsqrt(variance + EPS) * gain


def slot_ranks(device_of, groups):
    onehot = (device_of[:, None] == jnp.arange(groups, dtype=jnp.int32)[None, :]).astype(jnp.int32)
    before = jnp.cumsum(onehot, axis=0) - onehot
    return jnp.sum(before * onehot, axis=1)


def place_rows(values, target_slot, total_slots):
    row_ids = jnp.arange(values.shape[0], dtype=jnp.int32)
    source_index = jnp.zeros((total_slots,), jnp.int32).at[target_slot].set(row_ids)
    filled = jnp.zeros((total_slots,), jnp.bool_).at[target_slot].set(True)
    return jnp.where(filled[:, None], values[source_index], jnp.zeros((), values.dtype))


def shards(tokens, dest_pos, src_row, segment_ids, norm_gain, qkv_weight, qk_gain, out_weight):
    groups = lax.axis_size("dp")
    seq_length = tokens.shape[0]
    feat_cols = tokens.shape[1]
    capacity = 3 * seq_length // (2 * groups)
    send_device = dest_pos // seq_length
    send_slot = send_device * capacity + slot_ranks(send_device, groups)
    recv_device = src_row // seq_length
    recv_slot = recv_device * capacity + slot_ranks(recv_device, groups)
    outgoing = place_rows(tokens, send_slot, groups * capacity)
    arrived = lax.all_to_all(outgoing, "dp", split_axis=0, concat_axis=0, tiled=True)
    packed = arrived[recv_slot]
    head_width = qkv_weight.shape[2]
    head_count = head_width // HEAD_DIM
    values = packed.astype(jnp.float32)
    moments = lax.psum((jnp.sum(values, axis=1), jnp.sum(values * values, axis=1)), "mp")
    average = moments[0] / D
    variance = moments[1] / D - average * average
    gain_cols = lax.dynamic_slice_in_dim(norm_gain, lax.axis_index("mp") * feat_cols, feat_cols)
    normed_cols = (
        (values - average[:, None]) * lax.rsqrt(variance + EPS)[:, None] * gain_cols
    ).astype(jnp.bfloat16)
    projected = jnp.einsum(
        "td,cdw->ctw",
        lax.all_gather(normed_cols, "mp", axis=1, tiled=True),
        qkv_weight,
        preferred_element_type=jnp.float32,
    )
    shape = (seq_length, head_count, HEAD_DIM)
    query = norm_rows(projected[0].reshape(shape), qk_gain[0]).astype(jnp.bfloat16)
    key_norm = norm_rows(projected[1].reshape(shape), qk_gain[1]).astype(jnp.bfloat16)
    value = projected[2].reshape(shape).astype(jnp.bfloat16)
    scale = 1.0 / math.sqrt(HEAD_DIM)
    scores = jnp.einsum("qhd,khd->hqk", query, key_norm, preferred_element_type=jnp.float32) * scale
    allowed = segment_ids[:, None] == segment_ids[None, :]
    scores = jnp.where(allowed[None], scores, NEG)
    top = jnp.max(scores, axis=-1, keepdims=True)
    expo = jnp.exp(scores - top)
    weights = (expo / jnp.sum(expo, axis=-1, keepdims=True)).astype(jnp.bfloat16)
    context = jnp.einsum("hqk,khd->qhd", weights, value, preferred_element_type=jnp.float32)
    context = context.astype(jnp.bfloat16).reshape(seq_length, head_width)
    partial_value = jnp.dot(context, out_weight, preferred_element_type=jnp.float32)
    branch = lax.psum_scatter(
        partial_value.astype(jnp.bfloat16), "mp", scatter_dimension=1, tiled=True
    ).astype(jnp.float32)
    packed_out = (packed.astype(jnp.float32) + branch).astype(jnp.bfloat16)
    returning = place_rows(packed_out, recv_slot, groups * capacity)
    returned = lax.all_to_all(returning, "dp", split_axis=0, concat_axis=0, tiled=True)
    return returned[send_slot]


def solution(mesh):
    in_specs = (
        P("dp", "mp"),
        P("dp"),
        P("dp"),
        P("dp"),
        P(),
        P(None, None, "mp"),
        P(None, "mp", None),
        P("mp", None),
    )
    out_specs = P("dp", "mp")
    return jax.shard_map(shards, mesh=mesh, in_specs=in_specs, out_specs=out_specs, check_vma=False)
```

profile of v0, /device:TPU:0, one launch (start us, length us, event | category | flops | bytes accessed | tf_op | source)
XLA Modules:
  0.0 735.3 jit_solution(9280212939829577639)
XLA Ops:
  6.5 0.8 add_select_fusion
  7.4 2.3 reduce-window.16
  9.7 0.3 slice_reduce_fusion
  9.9 0.2 reduce-window.19
  10.1 0.1 add_bitcast_fusion
  10.2 1.3 broadcast_clamp_fusion
  11.5 4.3 scatter_custom_fusion.2
  15.9 0.6 copy-done.8
  16.4 4.3 scatter_custom_fusion.1
  20.8 0.1 broadcast_in_dim.72
  20.9 6.3 gather_fusion
  27.2 4.9 broadcast_select_fusion
  32.1 5.3 all-to-all-start
  37.4 0.0 all-gather.2.cloned.1.call-start
  37.5 2.3 reduce-window.14
  39.7 0.3 slice_reduce_fusion.1
  40.0 0.2 reduce-window.15
  40.2 0.8 dynamic_slice.3
  41.0 0.1 add_bitcast_fusion.1
  41.1 51.2 %all-to-all-done = bf16[8,192,1536]{2,1,0:T(8,128)(2,1)} async-done(((bf16[8,192,1536]{2,1,0:T(8,128)(2,1)}), bf16[8,192,1536]{2,1,0:T(8,128)(2,1)}, u32[]{:S(2)}, u32[]{:S(2)}) %all-to-all-start) | async-done | bytes 4718624 | tf_op jit(solution)/shard_map/all_to_all | solution.py:46
  92.3 9.6 %gather_fusion.1 = bf16[1024,1536]{1,0:T(8,128)(2,1)S(1)} fusion(bf16[1536,1536]{1,0:T(8,128)(2,1)} %bitcast.5, s32[1024]{0:T(1024)S(1)} %get-tuple-element.11), kind=kCustom, calls=%fused_computation.1 | custom fusion | bytes 6295552 | tf_op jit(solution)/shard_map/gather | solution.py:47
  101.9 1.0 convert_reduce_fusion
  102.9 12.9 %all-reduce = (f32[1024]{0:T(1024)S(1)}, f32[1024]{0:T(1024)S(1)}) all-reduce(f32[1024]{0:T(1024)S(1)} %get-tuple-element.6, f32[1024]{0:T(1024)S(1)} %get-tuple-element.5), channel_id=1, replica_groups=mesh['dp'=8,'mp'=4] {'mp'}, use_global_device_ids=true, to_apply=%region_12.13 | all-reduce | flops 2048 | bytes 16384 | tf_op jit(solution)/shard_map/psum | solution.py:51
  115.8 2.7 fusion.10
  118.5 0.0 reduce-scatter.2.cloned.1.call-start
  118.6 1.6 broadcast_compare_fusion
  120.3 213.1 %all-gather.2.cloned.1.call-done = bf16[1024,6144]{1,0:T(8,128)(2,1)} async-done(((bf16[1024,1536]{1,0:T(8,128)(2,1)}), bf16[1024,6144]{1,0:T(8,128)(2,1)}) %all-gather.2.cloned.1.call-update) | async-done | bytes 12582928 | tf_op jit(solution)/shard_map/all_gather | solution.py:60
  333.3 37.5 %fusion.13 = f32[3,1024,768]{1,2,0:T(8,128)} fusion(bf16[3,6144,768]{2,1,0:T(8,128)(2,1)} %param.13, bf16[1024,6144]{1,0:T(8,128)(2,1)} %all-gather.2.cloned.1.call-done), kind=kOutput, calls=%fused_computation.31 | convolution fusion | flops 28991029248 | bytes 50331648 | tf_op jit(solution)/shard_map/td,cdw->ctw/dot_general | solution.py:58
  370.8 3.3 slice.53
  374.1 5.6 fusion.44
  379.8 2.4 copy.14
  382.1 3.6 copy.16
  385.8 2.2 reduce_sum.87
  388.0 0.3 reduce_sum.85
  388.3 3.4 multiply_reduce_fusion
  391.7 1.8 multiply_reduce_fusion.1
  393.6 16.4 %fusion.46 = (f32[6,1024]{1,0:T(8,128)S(1)}, f32[6,1024,1024]{1,2,0:T(8,128)}) fusion(pred[1024,1024]{0,1:T(8,128)(4,1)} %broadcast_compare_fusion, f32[1024,6,128]{2,0,1:T(8,128)S(1)} %copy-done.3, f32[6,128]{1,0:T(8,128)S(1)} %get-tuple-element.26, f32[1024,6]{0,1:T(8,128)S(1)} %get-tuple-element.28, f32[1024,6]{0,1:T(8,128)S(1)} %broadcast_multiply_fusion.1, ...), kind=kOutput, calls=%fused_computation.103 | convolution fusion | flops 1642071040 | bytes 32634880 | tf_op jit(solution)/shard_map/sub | solution.py:73
  409.9 10.5 %fusion.18 = bf16[6,128,1024]{2,1,0:T(8,128)(2,1)S(1)} fusion(bf16[1024,6,128]{0,2,1:T(8,128)(2,1)} %bitcast.74, f32[6,1024,1024]{1,2,0:T(8,128)} %get-tuple-element.24, f32[6,1024]{1,0:T(8,128)S(1)} %get-tuple-element.23), kind=kOutput, calls=%fused_computation.39 | convolution fusion | flops 1623982080 | bytes 28336128 | tf_op jit(solution)/shard_map/hqk,khd->qhd/dot_general | solution.py:75
  420.4 16.0 %convolution_convert_fusion = bf16[1024,6144]{1,0:T(8,128)(2,1)} fusion(bf16[1024,768]{0,1:T(8,128)(2,1)S(1)} %bitcast.77, bf16[768,6144]{1,0:T(8,128)(2,1)} %param.15), kind=kOutput, calls=%fused_computation.19 | convolution fusion | flops 9669967872 | bytes 23592960 | tf_op jit(solution)/shard_map/dot_general | solution.py:77
  436.5 4.5 scatter_custom_fusion
  441.0 4.6 scatter_custom_fusion.3
  445.6 0.1 broadcast_in_dim.69
  445.7 201.0 %reduce-scatter.2.cloned.1.call-done = bf16[1024,1536]{1,0:T(8,128)(2,1)} async-done(((bf16[1024,6144]{1,0:T(8,128)(2,1)}), bf16[1024,1536]{1,0:T(8,128)(2,1)}) %reduce-scatter.2.cloned.1.call-update) | async-done | bytes 3145744 | tf_op jit(solution)/shard_map/reduce_scatter | solution.py:78
  646.7 3.7 fusion.12
  650.4 6.2 gather_fusion.2
  656.6 2.7 broadcast_select_fusion.1
  659.4 58.3 %all_to_all.18 = bf16[8,192,1536]{2,1,0:T(8,128)(2,1)} all-to-all(bf16[8,192,1536]{2,1,0:T(8,128)(2,1)S(1)} %broadcast_select_fusion.1), channel_id=1, replica_groups=mesh['dp'=8,'mp'=4] {'dp'}, dimensions={0} | all-to-all | bytes 9437184 | tf_op jit(solution)/shard_map/all_to_all | solution.py:83
  717.6 10.4 %gather_fusion.3 = bf16[1024,1536]{1,0:T(8,128)(2,1)} fusion(bf16[1536,1536]{1,0:T(8,128)(2,1)} %bitcast.67, s32[1024]{0:T(1024)S(1)} %copy-done.6), kind=kCustom, calls=%fused_computation.3 | custom fusion | bytes 6295552 | tf_op jit(solution)/shard_map/gather | solution.py:84
  (38 shorter events, 0.2 us)
Async XLA Ops:
  6.5 14.3 %copy-start = (bf16[1024,1536]{1,0:T(8,128)(2,1)S(1)}, bf16[1024,1536]{1,0:T(8,128)(2,1)}, u32[]{:S(2)}) copy-start(bf16[1024,1536]{1,0:T(8,128)(2,1)} %param.8) | copy-start | bytes 9437188
  15.9 0.6 copy-start.8
  32.1 5.4 copy-start.5
  32.1 60.2 %all-to-all-start = ((bf16[8,192,1536]{2,1,0:T(8,128)(2,1)}), bf16[8,192,1536]{2,1,0:T(8,128)(2,1)}, u32[]{:S(2)}, u32[]{:S(2)}) async-start(bf16[8,192,1536]{2,1,0:T(8,128)(2,1)} %broadcast_select_fusion), calls=%async_computation | async-start | bytes 9437184 | tf_op jit(solution)/shard_map/all_to_all | solution.py:46
  37.4 296.0 %all-gather.2.cloned.1.call-start = ((), (), s32[]{:S(2)}) async-start(), calls=%async_computation.3 | async-start | bytes 15728640 | tf_op jit(solution)/shard_map/all_gather | solution.py:60
  101.9 16.6 %copy-start.2 = (bf16[1024,1536]{1,0:T(8,128)(2,1)}, bf16[1024,1536]{1,0:T(8,128)(2,1)S(1)}, u32[]{:S(2)}) copy-start(bf16[1024,1536]{1,0:T(8,128)(2,1)S(1)} %gather_fusion.1) | copy-start | bytes 9437188
  115.8 2.8 copy-start.7
  115.8 2.8 copy-start.4
  118.5 528.2 %reduce-scatter.2.cloned.1.call-start = ((), (), s32[]{:S(2)}) async-start(), calls=%async_computation.4 | async-start | bytes 15728640 | tf_op jit(solution)/shard_map/reduce_scatter | solution.py:78
  388.3 3.4 copy-start.3
  659.4 58.3 %copy-start.6 = (s32[1024]{0:T(1024)S(1)}, s32[1024]{0:T(1024)}, u32[]{:S(2)}) copy-start(s32[1024]{0:T(1024)} %get-tuple-element.9) | copy-start | bytes 12292
  717.6 10.4 %copy-start.1 = (bf16[1024,1536]{1,0:T(8,128)(2,1)S(1)}, bf16[1024,1536]{1,0:T(8,128)(2,1)}, u32[]{:S(2)}) copy-start(bf16[1024,1536]{1,0:T(8,128)(2,1)} %param.8) | copy-start | bytes 9437188
Sparse Core Ops, SparseCore 0:
  118.6 214.6 all-gather.1
  436.6 210.0 reduce-scatter.1
where the time goes:
time: 744 us; the launch traced here: 735 us
  waiting for transfers between devices  465 us (62%)
  matrix products  80.4 us (11%)
  blocking collectives  71.1 us (10%)
  local copies, waits for them, and re-layouts  67.3 us (9%)
  other arithmetic  31.6 us (4%)
  between operations  14.2 us (2%)
    all_gather x1, waiting for transfers between devices, shards(): lax.all_gather(normed_cols, 'mp', axis=1, tiled=True)  213 us
    reduce_scatter x1, waiting for transfers between devices, shards(): lax.psum_scatter(partial_value.astype(jnp.bfloat16), 'mp', scatter_dimens...  201 us
    all_to_all x1, blocking collectives, shards(): lax.all_to_all(returning, 'dp', split_axis=0, concat_axis=0, tiled=True)  58.3 us
    all_to_all x1, waiting for transfers between devices, shards(): lax.all_to_all(outgoing, 'dp', split_axis=0, concat_axis=0, tiled=True)  51.2 us
    dot_general x1, matrix products, shards(): jnp.einsum('td,cdw->ctw', lax.all_gather(normed_cols, 'mp', axis=1, tiled...  37.5 us
    sub x1, matrix products, shards(): expo = jnp.exp(scores - top)  16.4 us
    dot_general x1, matrix products, shards(): jnp.dot(context, out_weight, preferred_element_type=jnp.float32)  16 us
  transfers between devices with their start and end apart: 3, of which 3 were waited for; matrix products, arithmetic and copies ran while one was open for 2% of the time, Pallas kernels for 0%

commit v1 on v0

v1 whole, which is shorter than its diff:
```python
import functools
import math

import jax
import jax.numpy as jnp
import numpy as np
from jax import lax
from jax.experimental import pallas as pl
from jax.experimental.pallas import tpu as pltpu
from jax.sharding import PartitionSpec as P

HEAD_DIM = 128
EPS = 1e-06
NEG = -1e30
VMEM = 56 * 1024 * 1024


def pick(total, wanted):
    return max(w for w in range(128, min(total, wanted) + 1, 128) if total % w == 0)


def line_schedule(n):
    steps = {}
    for s in range(1, n):
        for kind, low in (("E", 0), ("O", 1)):
            pairs = []
            for i in range(low, n - 1, 2):
                if i - s + 1 >= 0:
                    pairs.append((i, i + 1))
                if i + s <= n - 1:
                    pairs.append((i + 1, i))
            if pairs:
                steps[(s, kind)] = pairs
    slots = [[] for _ in range(n)]
    for (s, kind), pairs in sorted(steps.items()):
        for source, target in pairs:
            origin = target - s if source < target else target + s
            slots[target].append(((s, kind), origin))
    return steps, slots


def relay(block, axis, n):
    steps, slots = line_schedule(n)
    got = {}
    for s, kind in sorted(steps):
        other = "O" if kind == "E" else "E"
        source = block if s == 1 else got[(s - 1, other)]
        got[(s, kind)] = lax.ppermute(source, axis, steps[(s, kind)])
    place = lax.axis_index(axis)
    arrived = []
    for k in range(n - 1):
        keys = sorted({slots[i][k][0] for i in range(n)})
        value = got[keys[0]]
        for key in keys[1:]:
            here = np.array([slots[i][k][0] == key for i in range(n)])
            value = jnp.where(jnp.asarray(here)[place], got[key], value)
        arrived.append(value)
    return arrived


def origins(axis, n):
    _, slots = line_schedule(n)
    table = np.array([[slots[i][k][1] for k in range(n - 1)] for i in range(n)], np.int32)
    place = lax.axis_index(axis)
    return [jnp.asarray(table)[place, k] for k in range(n - 1)]


def project(x, weight, which, acc):
    rows, depth = x.shape
    kinds, _, width = weight.shape
    cols = pick(width, 384)

    def kernel(which_ref, x_ref, w_ref, *refs):
        part = jnp.dot(x_ref[...], w_ref[...], preferred_element_type=jnp.float32)
        if len(refs) == 2:
            part = part + refs[0][...]
        refs[-1][...] = part

    tile = pl.BlockSpec((None, rows, cols), lambda c, j, w: (c, 0, j))
    in_specs = [
        pl.BlockSpec((rows, depth), lambda c, j, w: (0, 0)),
        pl.BlockSpec((None, depth, cols), lambda c, j, w: (c, w[0], j)),
    ]
    args = [jnp.reshape(which, (1,)), x, weight]
    aliases = {}
    if acc is not None:
        in_specs.append(tile)
        args.append(acc)
        aliases = {3: 0}
    return pl.pallas_call(
        kernel,
        grid_spec=pltpu.PrefetchScalarGridSpec(
            num_scalar_prefetch=1,
            grid=(kinds, width // cols),
            in_specs=in_specs,
            out_specs=tile,
        ),
        out_shape=jax.ShapeDtypeStruct((kinds, rows, width), jnp.float32),
        input_output_aliases=aliases,
        compiler_params=pltpu.CompilerParams(vmem_limit_bytes=VMEM),
        cost_estimate=pl.CostEstimate(
            flops=2 * kinds * rows * depth * width,
            bytes_accessed=2 * kinds * depth * width + 8 * kinds * rows * width,
            transcendentals=0,
        ),
    )(*args)


def head_norm(values, gain):
    average = jnp.mean(values, axis=-1, keepdims=True)
    centred = values - average
    variance = jnp.mean(centred * centred, axis=-1, keepdims=True)
    return (centred * lax.rsqrt(variance + EPS) * gain).astype(jnp.bfloat16)


def attend(projected, gains, block_col, block_row, first, heads, reach):
    _, rows, width = projected.shape
    tile = pick(rows, 256)
    scale = 1.0 / math.sqrt(HEAD_DIM)

    def kernel(q_ref, k_ref, v_ref, gain_ref, col_ref, row_ref, out_ref):
        query = head_norm(q_ref[...], gain_ref[0:1, :])
        key = head_norm(k_ref[...], gain_ref[1:2, :])
        value = v_ref[...].astype(jnp.bfloat16)
        for begin in range(0, rows, tile):
            low = max(0, (begin - reach) // 128 * 128)
            high = min(rows, -(-(begin + tile + reach) // 128) * 128)
            scores = lax.dot_general(
                query[begin : begin + tile],
                key[low:high],
                (((1,), (1,)), ((), ())),
                preferred_element_type=jnp.float32,
            )
            same = col_ref[begin : begin + tile, :] == row_ref[:, low:high]
            scores = jnp.where(same, scores * scale, NEG)
            top = jnp.max(scores, axis=-1, keepdims=True)
            expo = jnp.exp(scores - top)
            total = jnp.sum(expo, axis=-1, keepdims=True)
            weights = (expo * (1.0 / total)).astype(jnp.bfloat16)
            context = jnp.dot(weights, value[low:high], preferred_element_type=jnp.float32)
            out_ref[begin : begin + tile, :] = context.astype(jnp.bfloat16)

    def part(c):
        return pl.BlockSpec((None, rows, HEAD_DIM), lambda h: (c, 0, first + h))

    return pl.pallas_call(
        kernel,
        grid=(heads,),
        in_specs=[
            part(0),
            part(1),
            part(2),
            pl.BlockSpec((None, 2, HEAD_DIM), lambda h: (first + h, 0, 0)),
            pl.BlockSpec((rows, 1), lambda h: (0, 0)),
            pl.BlockSpec((1, rows), lambda h: (0, 0)),
        ],
        out_specs=pl.BlockSpec((rows, HEAD_DIM), lambda h: (0, h)),
        out_shape=jax.ShapeDtypeStruct((rows, heads * HEAD_DIM), jnp.bfloat16),
        compiler_params=pltpu.CompilerParams(vmem_limit_bytes=VMEM),
        cost_estimate=pl.CostEstimate(
            flops=4 * heads * rows * rows * HEAD_DIM,
            bytes_accessed=14 * heads * rows * HEAD_DIM,
            transcendentals=heads * rows * rows,
        ),
    )(projected, projected, projected, gains, block_col, block_row)


def project_out(parts, weight, which, acc, residual):
    rows = parts[0].shape[0]
    _, depth, width = weight.shape
    cols = pick(width, 512)
    count = len(parts)

    def kernel(which_ref, *refs):
        out_ref = refs[-1]
        w_ref = refs[count]
        begin = 0
        total = None if acc is None else refs[count + 1][...]
        for x_ref in refs[:count]:
            depth_of = x_ref.shape[1]
            part = jnp.dot(
                x_ref[...], w_ref[begin : begin + depth_of, :], preferred_element_type=jnp.float32
            )
            total = part if total is None else total + part
            begin += depth_of
        if residual is not None:
            total = refs[-2][...].astype(jnp.float32) + total
        out_ref[...] = total.astype(out_ref.dtype)

    tile = pl.BlockSpec((rows, cols), lambda j, w: (0, j))
    in_specs = [pl.BlockSpec(p.shape, lambda j, w: (0, 0)) for p in parts]
    in_specs.append(pl.BlockSpec((None, depth, cols), lambda j, w: (w[0], 0, j)))
    args = [jnp.reshape(which, (1,)), *parts, weight]
    for extra in (acc, residual):
        if extra is not None:
            in_specs.append(tile)
            args.append(extra)
    out_type = jnp.float32 if residual is None else jnp.bfloat16
    return pl.pallas_call(
        kernel,
        grid_spec=pltpu.PrefetchScalarGridSpec(
            num_scalar_prefetch=1, grid=(width // cols,), in_specs=in_specs, out_specs=tile
        ),
        out_shape=jax.ShapeDtypeStruct((rows, width), out_type),
        compiler_params=pltpu.CompilerParams(vmem_limit_bytes=VMEM),
        cost_estimate=pl.CostEstimate(
            flops=2 * rows * depth * width,
            bytes_accessed=2 * depth * width + 8 * rows * width,
            transcendentals=0,
        ),
    )(*args)


def exchange_out_weight(out_weight, n, groups):
    depth, features = out_weight.shape
    place = lax.axis_index("mp")
    piece = depth // groups
    cols = features // n
    mine = lax.dynamic_slice_in_dim(out_weight, lax.axis_index("dp") * piece, piece, axis=0)

    def columns(index):
        return lax.dynamic_slice_in_dim(mine, index * cols, cols, axis=1)

    pieces = jnp.zeros((n, piece, cols), out_weight.dtype)
    pieces = lax.dynamic_update_slice_in_dim(pieces, columns(place)[None], place, axis=0)
    for d in range(1, n):
        sent = lax.ppermute(
            columns((place + d) % n), "mp", [(i, (i + d) % n) for i in range(n)]
        )
        pieces = lax.dynamic_update_slice_in_dim(pieces, sent[None], (place - d) % n, axis=0)
    return lax.all_gather(pieces, "dp", axis=1, tiled=True)


def shards(tokens, dest_pos, src_row, segment_ids, norm_gain, qkv_weight, qk_gain, out_weight):
    groups = lax.axis_size("dp")
    n = lax.axis_size("mp")
    place = lax.axis_index("mp")
    rows, cols = tokens.shape
    features = cols * n
    reach = 3 * rows // (2 * groups)
    heads = qkv_weight.shape[2] // HEAD_DIM

    segment = lax.all_gather(segment_ids, "dp", tiled=True)[dest_pos]
    block = dest_pos // rows * groups + segment
    block_col = block[:, None]
    block_row = block[None, :]
    gains = jnp.transpose(qk_gain, (1, 0, 2))

    with jax.named_scope("moments"):
        values = tokens.astype(jnp.float32)
        moments = lax.psum((jnp.sum(values, axis=1), jnp.sum(values * values, axis=1)), "mp")
        average = moments[0] / features
        inverse = lax.rsqrt(moments[1] / features - average * average + EPS)

    arrived = relay(tokens, "mp", n)
    sources = origins("mp", n)
    out_columns = exchange_out_weight(out_weight, n, groups)

    def normalize(block, origin):
        gain = lax.dynamic_slice_in_dim(norm_gain, origin * cols, cols)
        centred = block.astype(jnp.float32) - average[:, None]
        return (centred * inverse[:, None] * gain).astype(jnp.bfloat16)

    projected = None
    for block, origin in zip([tokens] + arrived, [place] + sources):
        with jax.named_scope("project"):
            projected = project(normalize(block, origin), qkv_weight, origin, projected)

    chunk = 2 if heads % 2 == 0 else 1
    contexts = []
    for first in range(0, heads, chunk):
        with jax.named_scope("attend"):
            contexts.append(
                attend(projected, gains, block_col, block_row, first, chunk, reach)
            )
    moved = [relay(context, "mp", n) for context in contexts]

    total = project_out(contexts, out_columns, place, None, None)
    for k in range(n - 1):
        last = k == n - 2
        total = project_out(
            [m[k] for m in moved], out_columns, sources[k], total, tokens if last else None
        )
    return total


def solution(mesh):
    in_specs = (
        P("dp", "mp"),
        P("dp"),
        P("dp"),
        P("dp"),
        P(),
        P(None, None, "mp"),
        P(None, "mp", None),
        P("mp", None),
    )
    out_specs = P("dp", "mp")
    return jax.shard_map(shards, mesh=mesh, in_specs=in_specs, out_specs=out_specs, check_vma=False)
```

time: 744 us -> 545 us (0.73)
  waiting for transfers between devices: 465 us -> 140 us
  Pallas kernels: 0 us -> 125 us
  blocking collectives: 71.1 us -> 193 us
  matrix products: 80.4 us -> 0 us
  local copies, waits for them, and re-layouts: 67.3 us -> 18.4 us
  starting transfers between devices: 5.38 us -> 30.1 us
  other arithmetic: 31.6 us -> 21.5 us
    all_gather x1, waiting for transfers between devices: 213 us -> 0.01 us  [exchange_out_weight(): return lax.all_gather(pieces, 'dp', axis=1, tiled=True)]
    reduce_scatter x1 -> x0, waiting for transfers between devices: 201 us -> none  [shards(): lax.psum_scatter(partial_value.astype(jnp.bfloat16), 'mp', scatter_dimens...]
    psum x1, blocking collectives: 12.9 us -> 184 us  [shards(): lax.psum((jnp.sum(values, axis=1), jnp.sum(values * values, axis=1)), 'mp')]
    ppermute x0 -> x23, waiting for transfers between devices: none -> 140 us  [the longest x3 78 us: exchange_out_weight(): lax.ppermute(columns((place + d) % n), 'mp', [(i, (i + d) % n) for i in r...]
    pallas_call x0 -> x11, Pallas kernels: none -> 125 us  [the longest x4 64.7 us: project(): pl.pallas_call(kernel, grid_spec=pltpu.PrefetchScalarGridSpec(num_scalar_...]
    dot_general x3 -> x0, matrix products: 64 us -> none  [the longest x1 37.5 us: shards(): jnp.einsum('td,cdw->ctw', lax.all_gather(normed_cols, 'mp', axis=1, tiled...]
    all_to_all x1 -> x0, blocking collectives: 58.3 us -> none  [shards(): lax.all_to_all(returning, 'dp', split_axis=0, concat_axis=0, tiled=True)]
    all_to_all x1 -> x0, waiting for transfers between devices: 51.2 us -> none  [shards(): lax.all_to_all(outgoing, 'dp', split_axis=0, concat_axis=0, tiled=True)]
  transfers between devices with their start and end apart: 3 -> 24, of which waited for: 3 -> 11; matrix products, arithmetic and copies ran while one was open for 2% -> 7% of each run, Pallas kernels for 0% -> 16%
where the time goes in v1:
time: 545 us; the launch traced here: 543 us
  blocking collectives  193 us (35%)
  waiting for transfers between devices  140 us (26%)
  Pallas kernels  125 us (23%)
  starting transfers between devices  30.1 us (6%)
  other arithmetic  21.5 us (4%)
  local copies, waits for them, and re-layouts  18.4 us (3%)
  between operations  15.5 us (3%)
    psum x1, blocking collectives, shards(): lax.psum((jnp.sum(values, axis=1), jnp.sum(values * values, axis=1)), 'mp')  184 us
    ppermute x3, waiting for transfers between devices, exchange_out_weight(): lax.ppermute(columns((place + d) % n), 'mp', [(i, (i + d) % n) for i in r...  78 us
    pallas_call x4, Pallas kernels, project(): pl.pallas_call(kernel, grid_spec=pltpu.PrefetchScalarGridSpec(num_scalar_...  64.7 us
    ppermute x20, waiting for transfers between devices, relay(): got[s, kind] = lax.ppermute(source, axis, steps[s, kind])  61.6 us
    pallas_call x4, Pallas kernels, project_out(): pl.pallas_call(kernel, grid_spec=pltpu.PrefetchScalarGridSpec(num_scalar_...  35.8 us
    pallas_call x3, Pallas kernels, attend(): pl.pallas_call(kernel, grid=(heads,), in_specs=[part(0), part(1), part(2)...  24.3 us
    ppermute x20, starting transfers between devices, relay(): got[s, kind] = lax.ppermute(source, axis, steps[s, kind])  24.2 us
    convert_element_type x1, other arithmetic, normalize(): return (centred * inverse[:, None] * gain).astype(jnp.bfloat16)  11.6 us
  transfers between devices with their start and end apart: 24, of which 11 were waited for; matrix products, arithmetic and copies ran while one was open for 7% of the time, Pallas kernels for 16%

profile of v1, /device:TPU:0, one launch (start us, length us, event | category | flops | bytes accessed | tf_op | source)
XLA Modules:
  0.0 543.1 jit_solution(7381218086294137688)
XLA Ops:
  6.6 2.7 fusion.9
  9.3 3.0 collective-permute-start.14
  12.3 1.6 collective-permute-start
  15.0 1.8 collective-permute-start.16
  17.8 1.8 bitcast_dynamic-update-slice_fusion.3
  19.7 3.0 collective-permute-done.14
  22.7 1.7 bitcast_dynamic-update-slice_fusion.2
  24.4 69.4 %collective-permute-done.15 = bf16[96,1536]{1,0:T(8,128)(2,1)} collective-permute-done((bf16[96,1536]{1,0:T(8,128)(2,1)}, bf16[96,1536]{1,0:T(8,128)(2,1)}, u32[]{:S(2)}, u32[]{:S(2)}) %collective-permute-start.15) | collective-permute-done | bytes 294944 | tf_op jit(solution)/shard_map/ppermute | solution.py:227
  93.8 1.7 bitcast_dynamic-update-slice_fusion.1
  95.5 5.6 %collective-permute-done.16 = bf16[96,1536]{1,0:T(8,128)(2,1)S(1)} collective-permute-done((bf16[96,1536]{1,0:T(8,128)(2,1)}, bf16[96,1536]{1,0:T(8,128)(2,1)S(1)}, u32[]{:S(2)}, u32[]{:S(2)}) %collective-permute-start.16) | collective-permute-done | bytes 294944 | tf_op jit(solution)/shard_map/ppermute | solution.py:227
  101.8 2.3 collective-permute-start.3
  104.1 2.4 collective-permute-start.1
  107.8 1.3 collective-permute-start.2
  112.2 9.2 %all_gather.6 = s32[8192]{0:T(1024)S(1)} all-gather(s32[1024]{0:T(1024)S(1)} %copy-done.8), channel_id=1, replica_groups=mesh['dp'=8,'mp'=4] {'dp'}, dimensions={0}, use_global_device_ids=true | all-gather | bytes 36864 | tf_op jit(solution)/shard_map/all_gather | solution.py:243
  121.4 6.2 %gather_fusion = s32[1024]{0:T(1024)S(1)} fusion(s32[8192]{0:T(1024)S(1)} %all_gather.6, s32[1024]{0:T(1024)S(1)} %fusion.7), kind=kCustom, calls=%fused_computation | custom fusion | bytes 12288 | tf_op jit(solution)/shard_map/gather | solution.py:243
  129.6 184.0 %all-reduce = (f32[1024]{0:T(1024)S(1)}, f32[1024]{0:T(1024)S(1)}) all-reduce(f32[1024]{0:T(1024)S(1)} %get-tuple-element.6, f32[1024]{0:T(1024)S(1)} %get-tuple-element.5), channel_id=1, replica_groups=mesh['dp'=8,'mp'=4] {'mp'}, use_global_device_ids=true, to_apply=%region_3.4 | all-reduce | flops 2048 | bytes 16384 | tf_op jit(solution)/shard_map/moments/psum | solution.py:251
  313.8 11.6 %fusion.3 = (bf16[1024,1536]{1,0:T(8,128)(2,1)}, bf16[1024,1536]{1,0:T(8,128)(2,1)}, bf16[1024,1536]{1,0:T(8,128)(2,1)}, bf16[1024,1536]{1,0:T(8,128)(2,1)}) fusion(bf16[1024,1536]{1,0:T(8,128)(2,1)S(1)} %copy-done, f32[1536]{0:T(1024)S(1)} %get-tuple-element.12, f32[1024]{0:T(1024)S(1)} %get-tuple-element.21, f32[1024]{0:T(1024)S(1)} %get-tuple-element.20, ...), kind=kLoop, calls=%fused_computation.7 | loop fusion | flops 34603008 | bytes 31490048 | tf_op jit(solution)/shard_map/project/convert_element_type | solution.py:262
  325.4 14.5 %project.4.refs_0_ = f32[3,1024,768]{2,1,0:T(8,128)} custom-call(s32[1]{0:T(128)} %bitcast.7.which_ref, bf16[1024,1536]{1,0:T(8,128)(2,1)} %get-tuple-element.16.x_ref, bf16[3,6144,768]{2,1,0:T(8,128)(2,1)} %w_ref.7), custom_call_target="tpu_custom_call" | custom-call | flops 7247757312 | bytes 25952256 | tf_op jit(solution)/shard_map/project/pallas_call | solution.py:90
  339.8 16.8 %project.5.refs_0_ = f32[3,1024,768]{2,1,0:T(8,128)} custom-call(s32[1]{0:T(128)} %bitcast.5.which_ref, bf16[1024,1536]{1,0:T(8,128)(2,1)} %get-tuple-element.18.x_ref, bf16[3,6144,768]{2,1,0:T(8,128)(2,1)} %w_ref.7, f32[3,1024,768]{2,1,0:T(8,128)} %project.4.refs_0_), custom_call_target="tpu_custom_call", output_to_operand_aliasing={{}: (3, {})} | custom-call | flops 7247757312 | bytes 25952256 | tf_op jit(solution)/shard_map/project/pallas_call | solution.py:90
  356.6 16.7 %project.6.refs_0_ = f32[3,1024,768]{2,1,0:T(8,128)} custom-call(s32[1]{0:T(128)} %bitcast.3.which_ref, bf16[1024,1536]{1,0:T(8,128)(2,1)} %get-tuple-element.17.x_ref, bf16[3,6144,768]{2,1,0:T(8,128)(2,1)} %w_ref.7, f32[3,1024,768]{2,1,0:T(8,128)} %project.5.refs_0_), custom_call_target="tpu_custom_call", output_to_operand_aliasing={{}: (3, {})} | custom-call | flops 7247757312 | bytes 25952256 | tf_op jit(solution)/shard_map/project/pallas_call | solution.py:90
  373.3 16.8 %project.7.q_ref.k_ref.v_ref = f32[3,1024,768]{2,1,0:T(8,128)} custom-call(s32[1]{0:T(128)} %bitcast.which_ref, bf16[1024,1536]{1,0:T(8,128)(2,1)} %get-tuple-element.19.x_ref, bf16[3,6144,768]{2,1,0:T(8,128)(2,1)} %w_ref.7, f32[3,1024,768]{2,1,0:T(8,128)} %project.6.refs_0_), custom_call_target="tpu_custom_call", output_to_operand_aliasing={{}: (3, {})} | custom-call | flops 7247757312 | bytes 25952256 | tf_op jit(solution)/shard_map/project/pallas_call | solution.py:90
  390.1 8.2 %attend.5.refs_2_ = bf16[1024,256]{1,0:T(8,128)(2,1)} custom-call(f32[3,1024,768]{2,1,0:T(8,128)} %project.7.q_ref.k_ref.v_ref, f32[3,1024,768]{2,1,0:T(8,128)} %project.7.q_ref.k_ref.v_ref, f32[3,1024,768]{2,1,0:T(8,128)} %project.7.q_ref.k_ref.v_ref, f32[6,2,128]{2,1,0:T(2,128)} %bitcast.23, s32[1024,1]{1,0:T(8,128)} %copy.23.col_ref, s32[1,1024]{1,0:T(1,128)} %bitcast.20), custom_call_target="tpu_custom_call" | custom-call | flops 1073741824 | bytes 3670016 | tf_op jit(solution)/shard_map/attend/pallas_call | solution.py:146
  399.2 8.2 %attend.4.refs_1_ = bf16[1024,256]{1,0:T(8,128)(2,1)} custom-call(f32[3,1024,768]{2,1,0:T(8,128)} %project.7.q_ref.k_ref.v_ref, f32[3,1024,768]{2,1,0:T(8,128)} %project.7.q_ref.k_ref.v_ref, f32[3,1024,768]{2,1,0:T(8,128)} %project.7.q_ref.k_ref.v_ref, f32[6,2,128]{2,1,0:T(2,128)} %bitcast.24, s32[1024,1]{1,0:T(8,128)} %copy.23.col_ref, s32[1,1024]{1,0:T(1,128)} %bitcast.21), custom_call_target="tpu_custom_call" | custom-call | flops 1073741824 | bytes 3670016 | tf_op jit(solution)/shard_map/attend/pallas_call | solution.py:146
  407.4 3.2 collective-permute-start.8
  410.6 8.0 %attend.3.refs_0_ = bf16[1024,256]{1,0:T(8,128)(2,1)} custom-call(f32[3,1024,768]{2,1,0:T(8,128)} %project.7.q_ref.k_ref.v_ref, f32[3,1024,768]{2,1,0:T(8,128)} %project.7.q_ref.k_ref.v_ref, f32[3,1024,768]{2,1,0:T(8,128)} %project.7.q_ref.k_ref.v_ref, f32[6,2,128]{2,1,0:T(2,128)} %bitcast.25, s32[1024,1]{1,0:T(8,128)} %copy.23.col_ref, s32[1,1024]{1,0:T(1,128)} %bitcast.22), custom_call_target="tpu_custom_call" | custom-call | flops 1073741824 | bytes 3670016 | tf_op jit(solution)/shard_map/attend/pallas_call | solution.py:146
  420.1 1.3 collective-permute-start.22
  421.4 1.6 collective-permute-done.8.refs_1_
  423.7 10.5 %collective-permute-done.5.refs_0_ = bf16[1024,256]{1,0:T(8,128)(2,1)S(1)} collective-permute-done((bf16[1024,256]{1,0:T(8,128)(2,1)}, bf16[1024,256]{1,0:T(8,128)(2,1)S(1)}, u32[]{:S(2)}, u32[]{:S(2)}) %collective-permute-start.5) | collective-permute-done | bytes 524320 | tf_op jit(solution)/shard_map/ppermute | solution.py:48
  435.7 1.3 collective-permute-start.20
  437.0 7.9 %collective-permute-done.22 = bf16[1024,256]{1,0:T(8,128)(2,1)S(1)} collective-permute-done((bf16[1024,256]{1,0:T(8,128)(2,1)S(1)}, bf16[1024,256]{1,0:T(8,128)(2,1)S(1)}, u32[]{:S(2)}, u32[]{:S(2)}) %collective-permute-start.22) | collective-permute-done | bytes 524320 | tf_op jit(solution)/shard_map/ppermute | solution.py:48
  446.2 1.3 collective-permute-start.13
  447.5 1.3 collective-permute-start.10
  448.8 1.3 collective-permute-start.7
  450.1 1.5 broadcast_select_fusion.refs_2_
  451.6 11.1 %collective-permute-done.20 = bf16[1024,256]{1,0:T(8,128)(2,1)S(1)} collective-permute-done((bf16[1024,256]{1,0:T(8,128)(2,1)S(1)}, bf16[1024,256]{1,0:T(8,128)(2,1)S(1)}, u32[]{:S(2)}, u32[]{:S(2)}) %collective-permute-start.20) | collective-permute-done | bytes 524320 | tf_op jit(solution)/shard_map/ppermute | solution.py:48
  462.7 1.5 broadcast_select_fusion.1.refs_1_
  464.2 9.7 %collective-permute-done.18 = bf16[1024,256]{1,0:T(8,128)(2,1)S(1)} collective-permute-done((bf16[1024,256]{1,0:T(8,128)(2,1)S(1)}, bf16[1024,256]{1,0:T(8,128)(2,1)S(1)}, u32[]{:S(2)}, u32[]{:S(2)}) %collective-permute-start.18) | collective-permute-done | bytes 524320 | tf_op jit(solution)/shard_map/ppermute | solution.py:48
  473.9 1.5 broadcast_select_fusion.2.refs_0_
  475.4 9.8 %collective-permute-done.13 = bf16[1024,256]{1,0:T(8,128)(2,1)S(1)} collective-permute-done((bf16[1024,256]{1,0:T(8,128)(2,1)S(1)}, bf16[1024,256]{1,0:T(8,128)(2,1)S(1)}, u32[]{:S(2)}, u32[]{:S(2)}) %collective-permute-start.13) | collective-permute-done | bytes 524320 | tf_op jit(solution)/shard_map/ppermute | solution.py:48
  485.2 1.5 broadcast_select_fusion.3.refs_2_
  486.7 6.8 %collective-permute-done.10 = bf16[1024,256]{1,0:T(8,128)(2,1)S(1)} collective-permute-done((bf16[1024,256]{1,0:T(8,128)(2,1)S(1)}, bf16[1024,256]{1,0:T(8,128)(2,1)S(1)}, u32[]{:S(2)}, u32[]{:S(2)}) %collective-permute-start.10) | collective-permute-done | bytes 524320 | tf_op jit(solution)/shard_map/ppermute | solution.py:48
  493.4 1.5 broadcast_select_fusion.4.refs_1_
  494.9 4.1 collective-permute-done.7
  499.0 1.5 broadcast_select_fusion.5.refs_0_
  500.5 6.8 %shard_map.154.refs_4_ = f32[1024,1536]{1,0:T(8,128)} custom-call(s32[1]{0:T(128)} %bitcast.7.which_ref, bf16[1024,256]{1,0:T(8,128)(2,1)} %attend.3.refs_0_, bf16[1024,256]{1,0:T(8,128)(2,1)} %attend.4.refs_1_, bf16[1024,256]{1,0:T(8,128)(2,1)} %attend.5.refs_2_, bf16[4,768,1536]{2,1,0:T(8,128)(2,1)} %all-gather.2.cloned.1.call-done.refs_3_), custom_call_target="tpu_custom_call" | custom-call | flops 2415919104 | bytes 14942208 | tf_op jit(solution)/shard_map/pallas_call | solution.py:199
  507.3 9.6 %shard_map.155.refs_4_ = f32[1024,1536]{1,0:T(8,128)} custom-call(s32[1]{0:T(128)} %bitcast.5.which_ref, bf16[1024,256]{1,0:T(8,128)(2,1)} %copy-done.4, bf16[1024,256]{1,0:T(8,128)(2,1)} %copy-done.3, bf16[1024,256]{1,0:T(8,128)(2,1)} %copy-done.2, bf16[4,768,1536]{2,1,0:T(8,128)(2,1)} %all-gather.2.cloned.1.call-done.refs_3_, f32[1024,1536]{1,0:T(8,128)} %shard_map.154.refs_4_), custom_call_target="tpu_custom_call" | custom-call | flops 2415919104 | bytes 14942208 | tf_op jit(solution)/shard_map/pallas_call | solution.py:199
  516.9 9.6 %shard_map.156.refs_4_ = f32[1024,1536]{1,0:T(8,128)} custom-call(s32[1]{0:T(128)} %bitcast.3.which_ref, bf16[1024,256]{1,0:T(8,128)(2,1)} %broadcast_select_fusion.2.refs_0_, bf16[1024,256]{1,0:T(8,128)(2,1)} %broadcast_select_fusion.1.refs_1_, bf16[1024,256]{1,0:T(8,128)(2,1)} %broadcast_select_fusion.refs_2_, ...), custom_call_target="tpu_custom_call" | custom-call | flops 2415919104 | bytes 14942208 | tf_op jit(solution)/shard_map/pallas_call | solution.py:199
  526.5 9.8 %shard_map.157 = bf16[1024,1536]{1,0:T(8,128)(2,1)} custom-call(s32[1]{0:T(128)} %bitcast.which_ref, bf16[1024,256]{1,0:T(8,128)(2,1)} %broadcast_select_fusion.5.refs_0_, bf16[1024,256]{1,0:T(8,128)(2,1)} %broadcast_select_fusion.4.refs_1_, bf16[1024,256]{1,0:T(8,128)(2,1)} %broadcast_select_fusion.3.refs_2_, ...), custom_call_target="tpu_custom_call" | custom-call | flops 2415919104 | bytes 14942208 | tf_op jit(solution)/shard_map/pallas_call | solution.py:199
  (58 shorter events, 13.4 us)
Async XLA Ops:
  6.5 494.0 %all-gather.2.cloned.1.call-start = ((), (), s32[]{:S(2)}) async-start(), calls=%async_computation | async-start | bytes 10616832 | tf_op jit(solution)/shard_map/all_gather | solution.py:231
  6.5 95.3 %copy-start = (bf16[1024,1536]{1,0:T(8,128)(2,1)S(1)}, bf16[1024,1536]{1,0:T(8,128)(2,1)}, u32[]{:S(2)}) copy-start(bf16[1024,1536]{1,0:T(8,128)(2,1)} %refs_5_.1) | copy-start | bytes 9437188
  6.5 102.6 %copy-start.9 = (s32[4,3]{1,0:T(4,128)S(1)}, s32[4,3]{1,0:T(4,128)}, u32[]{:S(2)}) copy-start(s32[4,3]{1,0:T(4,128)} %constant.141.clone) | copy-start | bytes 148
  6.5 105.0 %copy-start.10 = (pred[4]{0:T(512)(128)(4,1)S(1)}, pred[4]{0:T(512)(128)(4,1)}, u32[]{:S(2)}) copy-start(pred[4]{0:T(512)(128)(4,1)} %constant.140.clone) | copy-start | bytes 16
  6.5 105.7 %copy-start.8 = (s32[1024]{0:T(1024)S(1)}, s32[1024]{0:T(1024)}, u32[]{:S(2)}) copy-start(s32[1024]{0:T(1024)} %param.19) | copy-start | bytes 12292
  6.5 114.8 %copy-start.7 = (s32[1024]{0:T(1024)S(1)}, s32[1024]{0:T(1024)}, u32[]{:S(2)}) copy-start(s32[1024]{0:T(1024)} %param.18) | copy-start | bytes 12292
  9.3 13.4 %collective-permute-start.14 = (bf16[96,1536]{1,0:T(8,128)(2,1)}, bf16[96,1536]{1,0:T(8,128)(2,1)}, u32[]{:S(2)}, u32[]{:S(2)}) collective-permute-start(bf16[96,1536]{1,0:T(8,128)(2,1)} %get-tuple-element.10), channel_id=1, source_target_pairs={{0,1},{1,2},{2,3},{3,0},{4,5},{5,6},{6,7},{7,4},{8,9},{9,10},{10,1... | collective-permute-start | bytes 884744 | tf_op jit(solution)/shard_map/ppermute | solution.py:227
  12.3 91.8 %collective-permute-start = (bf16[1024,1536]{1,0:T(8,128)(2,1)}, bf16[1024,1536]{1,0:T(8,128)(2,1)}, u32[]{:S(2)}, u32[]{:S(2)}) collective-permute-start(bf16[1024,1536]{1,0:T(8,128)(2,1)} %refs_5_.1), channel_id=1, source_target_pairs={{0,1},{1,0},{2,3},{3,2},{4,5},{5,4},{6,7},{7,6},{8,9},{9,8},{10,11... | collective-permute-start | bytes 9437192 | tf_op jit(solution)/shard_map/ppermute | solution.py:48
  13.9 79.9 %collective-permute-start.15 = (bf16[96,1536]{1,0:T(8,128)(2,1)}, bf16[96,1536]{1,0:T(8,128)(2,1)}, u32[]{:S(2)}, u32[]{:S(2)}) collective-permute-start(bf16[96,1536]{1,0:T(8,128)(2,1)} %get-tuple-element.11), channel_id=1, source_target_pairs={{0,2},{1,3},{2,0},{3,1},{4,6},{5,7},{6,4},{7,5},{8,10},{9,11},{10,... | collective-permute-start | bytes 884744 | tf_op jit(solution)/shard_map/ppermute | solution.py:227
  15.0 86.1 %collective-permute-start.16 = (bf16[96,1536]{1,0:T(8,128)(2,1)}, bf16[96,1536]{1,0:T(8,128)(2,1)S(1)}, u32[]{:S(2)}, u32[]{:S(2)}) collective-permute-start(bf16[96,1536]{1,0:T(8,128)(2,1)} %get-tuple-element.9), channel_id=1, source_target_pairs={{0,3},{1,0},{2,1},{3,2},{4,7},{5,4},{6,5},{7,6},{8,11},{9,8},{10,9... | collective-permute-start | bytes 884744 | tf_op jit(solution)/shard_map/ppermute | solution.py:227
  101.8 4.7 collective-permute-start.3
  104.1 3.7 collective-permute-start.1
  106.5 207.3 %collective-permute-start.4 = (bf16[1024,1536]{1,0:T(8,128)(2,1)}, bf16[1024,1536]{1,0:T(8,128)(2,1)}, u32[]{:S(2)}, u32[]{:S(2)}) collective-permute-start(bf16[1024,1536]{1,0:T(8,128)(2,1)} %collective-permute-done.3), channel_id=1, source_target_pairs={{1,0},{2,3},{5,4},{6,7},{9,8},{10,11},{13,12},{14,15},{17,16},{18,... | collective-permute-start | bytes 9437192 | tf_op jit(solution)/shard_map/ppermute | solution.py:48
  107.8 206.0 %collective-permute-start.2 = (bf16[1024,1536]{1,0:T(8,128)(2,1)}, bf16[1024,1536]{1,0:T(8,128)(2,1)}, u32[]{:S(2)}, u32[]{:S(2)}) collective-permute-start(bf16[1024,1536]{1,0:T(8,128)(2,1)} %collective-permute-done.1), channel_id=1, source_target_pairs={{1,0},{2,3},{5,4},{6,7},{9,8},{10,11},{13,12},{14,15},{17,16},{18,... | collective-permute-start | bytes 9437192 | tf_op jit(solution)/shard_map/ppermute | solution.py:48
  121.4 192.3 %copy-start.6 = (f32[6144]{0:T(1024)S(1)}, f32[6144]{0:T(1024)}, u32[]{:S(2)}) copy-start(f32[6144]{0:T(1024)} %param.20) | copy-start | bytes 73732
  127.6 197.8 %copy-start.5 = (s32[1024]{0:T(1024)}, s32[1024]{0:T(1024)S(1)}, u32[]{:S(2)}) copy-start(s32[1024]{0:T(1024)S(1)} %fusion.6) | copy-start | bytes 12292
  398.3 21.1 %collective-permute-start.11 = (bf16[1024,256]{1,0:T(8,128)(2,1)}, bf16[1024,256]{1,0:T(8,128)(2,1)S(1)}, u32[]{:S(2)}, u32[]{:S(2)}) collective-permute-start(bf16[1024,256]{1,0:T(8,128)(2,1)} %attend.5.refs_2_), channel_id=1, source_target_pairs={{0,1},{1,0},{2,3},{3,2},{4,5},{5,4},{6,7},{7,6},{8,9},{9,8},{10,11... | collective-permute-start | bytes 1572872 | tf_op jit(solution)/shard_map/ppermute | solution.py:48
  398.3 21.8 %collective-permute-start.21 = (bf16[1024,256]{1,0:T(8,128)(2,1)}, bf16[1024,256]{1,0:T(8,128)(2,1)S(1)}, u32[]{:S(2)}, u32[]{:S(2)}) collective-permute-start(bf16[1024,256]{1,0:T(8,128)(2,1)} %attend.5.refs_2_), channel_id=1, source_target_pairs={{1,2},{2,1},{5,6},{6,5},{9,10},{10,9},{13,14},{14,13},{17,18},{18,... | collective-permute-start | bytes 1572872 | tf_op jit(solution)/shard_map/ppermute | solution.py:48
  407.4 11.3 %copy-start.1 = (bf16[1024,256]{1,0:T(8,128)(2,1)S(1)}, bf16[1024,256]{1,0:T(8,128)(2,1)}, u32[]{:S(2)}) copy-start(bf16[1024,256]{1,0:T(8,128)(2,1)} %attend.4.refs_1_) | copy-start | bytes 1572868
  407.4 15.7 %collective-permute-start.8 = (bf16[1024,256]{1,0:T(8,128)(2,1)}, bf16[1024,256]{1,0:T(8,128)(2,1)S(1)}, u32[]{:S(2)}, u32[]{:S(2)}) collective-permute-start(bf16[1024,256]{1,0:T(8,128)(2,1)} %attend.4.refs_1_), channel_id=1, source_target_pairs={{0,1},{1,0},{2,3},{3,2},{4,5},{5,4},{6,7},{7,6},{8,9},{9,8},{10,11... | collective-permute-start | bytes 1572872 | tf_op jit(solution)/shard_map/ppermute | solution.py:48
  418.6 15.7 %collective-permute-start.5 = (bf16[1024,256]{1,0:T(8,128)(2,1)}, bf16[1024,256]{1,0:T(8,128)(2,1)S(1)}, u32[]{:S(2)}, u32[]{:S(2)}) collective-permute-start(bf16[1024,256]{1,0:T(8,128)(2,1)} %attend.3.refs_0_), channel_id=1, source_target_pairs={{0,1},{1,0},{2,3},{3,2},{4,5},{5,4},{6,7},{7,6},{8,9},{9,8},{10,11... | collective-permute-start | bytes 1572872 | tf_op jit(solution)/shard_map/ppermute | solution.py:48
  418.7 16.3 %collective-permute-start.19 = (bf16[1024,256]{1,0:T(8,128)(2,1)S(1)}, bf16[1024,256]{1,0:T(8,128)(2,1)S(1)}, u32[]{:S(2)}, u32[]{:S(2)}) collective-permute-start(bf16[1024,256]{1,0:T(8,128)(2,1)S(1)} %copy-done.1), channel_id=1, source_target_pairs={{1,2},{2,1},{5,6},{6,5},{9,10},{10,9},{13,14},{14,13},{17,18},{18,... | collective-permute-start | bytes 1572872 | tf_op jit(solution)/shard_map/ppermute | solution.py:48
  419.4 67.3 %copy-start.2 = (bf16[1024,256]{1,0:T(8,128)(2,1)}, bf16[1024,256]{1,0:T(8,128)(2,1)S(1)}, u32[]{:S(2)}) copy-start(bf16[1024,256]{1,0:T(8,128)(2,1)S(1)} %collective-permute-done.11.refs_2_) | copy-start | bytes 1572868
  419.4 16.3 %collective-permute-start.17 = (bf16[1024,256]{1,0:T(8,128)(2,1)}, bf16[1024,256]{1,0:T(8,128)(2,1)S(1)}, u32[]{:S(2)}, u32[]{:S(2)}) collective-permute-start(bf16[1024,256]{1,0:T(8,128)(2,1)} %attend.3.refs_0_), channel_id=1, source_target_pairs={{1,2},{2,1},{5,6},{6,5},{9,10},{10,9},{13,14},{14,13},{17,18},{18,... | collective-permute-start | bytes 1572872 | tf_op jit(solution)/shard_map/ppermute | solution.py:48
  420.1 24.8 %collective-permute-start.22 = (bf16[1024,256]{1,0:T(8,128)(2,1)S(1)}, bf16[1024,256]{1,0:T(8,128)(2,1)S(1)}, u32[]{:S(2)}, u32[]{:S(2)}) collective-permute-start(bf16[1024,256]{1,0:T(8,128)(2,1)S(1)} %collective-permute-done.21), channel_id=1, source_target_pairs={{1,0},{2,3},{5,4},{6,7},{9,8},{10,11},{13,12},{14,15},{17,16},{18,... | collective-permute-start | bytes 1572872 | tf_op jit(solution)/shard_map/ppermute | solution.py:48
  423.0 63.6 %copy-start.3 = (bf16[1024,256]{1,0:T(8,128)(2,1)}, bf16[1024,256]{1,0:T(8,128)(2,1)S(1)}, u32[]{:S(2)}) copy-start(bf16[1024,256]{1,0:T(8,128)(2,1)S(1)} %collective-permute-done.8.refs_1_) | copy-start | bytes 1572868
  423.0 23.1 %collective-permute-start.12 = (bf16[1024,256]{1,0:T(8,128)(2,1)S(1)}, bf16[1024,256]{1,0:T(8,128)(2,1)S(1)}, u32[]{:S(2)}, u32[]{:S(2)}) collective-permute-start(bf16[1024,256]{1,0:T(8,128)(2,1)S(1)} %collective-permute-done.11.refs_2_), channel_id=1, source_target_pairs={{1,2},{2,1},{5,6},{6,5},{9,10},{10,9},{13,14},{14,13},{17,18},{18,... | collective-permute-start | bytes 1572872 | tf_op jit(solution)/shard_map/ppermute | solution.py:48
  434.3 52.4 %copy-start.4 = (bf16[1024,256]{1,0:T(8,128)(2,1)}, bf16[1024,256]{1,0:T(8,128)(2,1)S(1)}, u32[]{:S(2)}) copy-start(bf16[1024,256]{1,0:T(8,128)(2,1)S(1)} %collective-permute-done.5.refs_0_) | copy-start | bytes 1572868
  434.3 13.2 %collective-permute-start.9 = (bf16[1024,256]{1,0:T(8,128)(2,1)S(1)}, bf16[1024,256]{1,0:T(8,128)(2,1)S(1)}, u32[]{:S(2)}, u32[]{:S(2)}) collective-permute-start(bf16[1024,256]{1,0:T(8,128)(2,1)S(1)} %collective-permute-done.8.refs_1_), channel_id=1, source_target_pairs={{1,2},{2,1},{5,6},{6,5},{9,10},{10,9},{13,14},{14,13},{17,18},{18,... | collective-permute-start | bytes 1572872 | tf_op jit(solution)/shard_map/ppermute | solution.py:48
  435.0 13.8 %collective-permute-start.6 = (bf16[1024,256]{1,0:T(8,128)(2,1)S(1)}, bf16[1024,256]{1,0:T(8,128)(2,1)S(1)}, u32[]{:S(2)}, u32[]{:S(2)}) collective-permute-start(bf16[1024,256]{1,0:T(8,128)(2,1)S(1)} %collective-permute-done.5.refs_0_), channel_id=1, source_target_pairs={{1,2},{2,1},{5,6},{6,5},{9,10},{10,9},{13,14},{14,13},{17,18},{18,... | collective-permute-start | bytes 1572872 | tf_op jit(solution)/shard_map/ppermute | solution.py:48
  435.7 27.0 %collective-permute-start.20 = (bf16[1024,256]{1,0:T(8,128)(2,1)S(1)}, bf16[1024,256]{1,0:T(8,128)(2,1)S(1)}, u32[]{:S(2)}, u32[]{:S(2)}) collective-permute-start(bf16[1024,256]{1,0:T(8,128)(2,1)S(1)} %collective-permute-done.19), channel_id=1, source_target_pairs={{1,0},{2,3},{5,4},{6,7},{9,8},{10,11},{13,12},{14,15},{17,16},{18,... | collective-permute-start | bytes 1572872 | tf_op jit(solution)/shard_map/ppermute | solution.py:48
  444.9 29.1 %collective-permute-start.18 = (bf16[1024,256]{1,0:T(8,128)(2,1)S(1)}, bf16[1024,256]{1,0:T(8,128)(2,1)S(1)}, u32[]{:S(2)}, u32[]{:S(2)}) collective-permute-start(bf16[1024,256]{1,0:T(8,128)(2,1)S(1)} %collective-permute-done.17), channel_id=1, source_target_pairs={{1,0},{2,3},{5,4},{6,7},{9,8},{10,11},{13,12},{14,15},{17,16},{18,... | collective-permute-start | bytes 1572872 | tf_op jit(solution)/shard_map/ppermute | solution.py:48
  446.2 39.0 %collective-permute-start.13 = (bf16[1024,256]{1,0:T(8,128)(2,1)S(1)}, bf16[1024,256]{1,0:T(8,128)(2,1)S(1)}, u32[]{:S(2)}, u32[]{:S(2)}) collective-permute-start(bf16[1024,256]{1,0:T(8,128)(2,1)S(1)} %collective-permute-done.12), channel_id=1, source_target_pairs={{1,0},{2,3},{5,4},{6,7},{9,8},{10,11},{13,12},{14,15},{17,16},{18,... | collective-permute-start | bytes 1572872 | tf_op jit(solution)/shard_map/ppermute | solution.py:48
  447.5 45.9 %collective-permute-start.10 = (bf16[1024,256]{1,0:T(8,128)(2,1)S(1)}, bf16[1024,256]{1,0:T(8,128)(2,1)S(1)}, u32[]{:S(2)}, u32[]{:S(2)}) collective-permute-start(bf16[1024,256]{1,0:T(8,128)(2,1)S(1)} %collective-permute-done.9), channel_id=1, source_target_pairs={{1,0},{2,3},{5,4},{6,7},{9,8},{10,11},{13,12},{14,15},{17,16},{18,... | collective-permute-start | bytes 1572872 | tf_op jit(solution)/shard_map/ppermute | solution.py:48
  448.8 50.2 %collective-permute-start.7 = (bf16[1024,256]{1,0:T(8,128)(2,1)S(1)}, bf16[1024,256]{1,0:T(8,128)(2,1)S(1)}, u32[]{:S(2)}, u32[]{:S(2)}) collective-permute-start(bf16[1024,256]{1,0:T(8,128)(2,1)S(1)} %collective-permute-done.6), channel_id=1, source_target_pairs={{1,0},{2,3},{5,4},{6,7},{9,8},{10,11},{13,12},{14,15},{17,16},{18,... | collective-permute-start | bytes 1572872 | tf_op jit(solution)/shard_map/ppermute | solution.py:48
Sparse Core Ops, SparseCore 0:
  101.9 58.7 all-gather.1

commit v2 on v1

v2 whole, which is shorter than its diff:
```python
import functools
import math

import jax
import jax.numpy as jnp
import numpy as np
from jax import lax
from jax.experimental import pallas as pl
from jax.experimental.pallas import tpu as pltpu
from jax.sharding import PartitionSpec as P

HEAD_DIM = 128
EPS = 1e-06
NEG = -1e30
VMEM = 56 * 1024 * 1024
COST = pl.CostEstimate(flops=1024, bytes_accessed=1024, transcendentals=0)


def pick(total, wanted):
    return max(w for w in range(128, min(total, wanted) + 1, 128) if total % w == 0)


def line_schedule(n):
    steps = {}
    for s in range(1, n):
        for kind, low in (("E", 0), ("O", 1)):
            pairs = []
            for i in range(low, n - 1, 2):
                if i - s + 1 >= 0:
                    pairs.append((i, i + 1))
                if i + s <= n - 1:
                    pairs.append((i + 1, i))
            if pairs:
                steps[(s, kind)] = pairs
    slots = [[] for _ in range(n)]
    for (s, kind), pairs in sorted(steps.items()):
        for source, target in pairs:
            origin = target - s if source < target else target + s
            slots[target].append(((s, kind), origin))
    return steps, slots


class Relay:
    def __init__(self, block, axis, n):
        self.axis, self.n = axis, n
        self.steps, self.slots = line_schedule(n)
        self.got = {(0, "E"): block, (0, "O"): block}

    def step(self, s, *after):
        kinds = [kind for kind in "EO" if (s, kind) in self.steps]
        sources = [self.got[(s - 1, "O" if kind == "E" else "E")] for kind in kinds]
        sources = lax.optimization_barrier((*sources, *after))
        for kind, source in zip(kinds, sources):
            self.got[(s, kind)] = lax.ppermute(source, self.axis, self.steps[(s, kind)])

    def arrived(self, k):
        keys = sorted({slot[k][0] for slot in self.slots})
        if all({key for key, _ in slot} & set(keys) == {slot[k][0]} for slot in self.slots):
            return [self.got[key] for key in keys]
        place = lax.axis_index(self.axis)
        value = self.got[keys[0]]
        for key in keys[1:]:
            here = np.array([slot[k][0] == key for slot in self.slots])
            value = jnp.where(jnp.asarray(here)[place], self.got[key], value)
        return [value]


def origins(axis, n):
    _, slots = line_schedule(n)
    table = np.array([[slots[i][k][1] for k in range(n - 1)] for i in range(n)], np.int32)
    place = lax.axis_index(axis)
    return [jnp.asarray(table)[place, k] for k in range(n - 1)]


def whole(refs):
    value = refs[0][...]
    for ref in refs[1:]:
        value = value + ref[...]
    return value


def project(parts, weight, which, acc):
    rows, depth = parts[0].shape
    kinds, _, width = weight.shape
    cols = pick(width, 768)
    count = len(parts)

    def kernel(which_ref, *refs):
        x = whole(refs[:count])
        part = jnp.dot(x, refs[count][...], preferred_element_type=jnp.float32)
        if acc is not None:
            part = part + refs[count + 1][...]
        refs[-1][...] = part

    tile = pl.BlockSpec((None, rows, cols), lambda c, j, w: (c, 0, j))
    in_specs = [pl.BlockSpec((rows, depth), lambda c, j, w: (0, 0)) for _ in parts]
    in_specs.append(pl.BlockSpec((None, depth, cols), lambda c, j, w: (c, w[0], j)))
    args = [jnp.reshape(which, (1,)), *parts, weight]
    aliases = {}
    if acc is not None:
        in_specs.append(tile)
        args.append(acc)
        aliases = {count + 2: 0}
    return pl.pallas_call(
        kernel,
        grid_spec=pltpu.PrefetchScalarGridSpec(
            num_scalar_prefetch=1,
            grid=(kinds, width // cols),
            in_specs=in_specs,
            out_specs=tile,
        ),
        out_shape=jax.ShapeDtypeStruct((kinds, rows, width), jnp.float32),
        input_output_aliases=aliases,
        compiler_params=pltpu.CompilerParams(vmem_limit_bytes=VMEM),
        cost_estimate=pl.CostEstimate(
            flops=2 * kinds * rows * depth * width,
            bytes_accessed=2 * kinds * depth * width + 8 * kinds * rows * width,
            transcendentals=0,
        ),
    )(*args)


def head_norm(values, gain):
    average = jnp.mean(values, axis=-1, keepdims=True)
    centred = values - average
    variance = jnp.mean(centred * centred, axis=-1, keepdims=True)
    return (centred * lax.rsqrt(variance + EPS) * gain).astype(jnp.bfloat16)


def attend(parts, weight, which, acc, gains, block_col, block_row, first, heads, reach):
    rows, depth = parts[0].shape
    kinds = weight.shape[0]
    cols = heads * HEAD_DIM
    deep = pick(depth, 512)
    steps = depth // deep
    tile = pick(rows, 256)
    scale = 1.0 / math.sqrt(HEAD_DIM)
    count = len(parts)

    def one_head(q, k, v, gain, col_ref, row_ref, out_ref, place):
        query = head_norm(q, gain[0:1, :])
        key = head_norm(k, gain[1:2, :])
        value = v.astype(jnp.bfloat16)
        for begin in range(0, rows, tile):
            low = max(0, (begin - reach) // 128 * 128)
            high = min(rows, -(-(begin + tile + reach) // 128) * 128)
            scores = lax.dot_general(
                query[begin : begin + tile],
                key[low:high],
                (((1,), (1,)), ((), ())),
                preferred_element_type=jnp.float32,
            )
            same = col_ref[begin : begin + tile, :] == row_ref[:, low:high]
            scores = jnp.where(same, scores * scale, NEG)
            top = jnp.max(scores, axis=-1, keepdims=True)
            expo = jnp.exp(scores - top)
            total = jnp.sum(expo, axis=-1, keepdims=True)
            weights = (expo * (1.0 / total)).astype(jnp.bfloat16)
            context = jnp.dot(weights, value[low:high], preferred_element_type=jnp.float32)
            out_ref[begin : begin + tile, place : place + HEAD_DIM] = context.astype(jnp.bfloat16)

    def kernel(which_ref, *refs):
        x_refs = refs[:count]
        w_refs = refs[count : count + kinds]
        acc_refs = refs[count + kinds : count + 2 * kinds]
        gain_ref, col_ref, row_ref, out_ref, held = refs[count + 2 * kinds :]
        step = pl.program_id(0)
        x = whole(x_refs)

        @pl.when(step == 0)
        def _():
            for c in range(kinds):
                held[c] = acc_refs[c][...] + jnp.dot(
                    x, w_refs[c][...], preferred_element_type=jnp.float32
                )

        @pl.when(step > 0)
        def _():
            for c in range(kinds):
                held[c] += jnp.dot(x, w_refs[c][...], preferred_element_type=jnp.float32)

        @pl.when(step == steps - 1)
        def _():
            for h in range(heads):
                at = slice(h * HEAD_DIM, (h + 1) * HEAD_DIM)
                one_head(
                    held[0, :, at], held[1, :, at], held[2, :, at], gain_ref[h],
                    col_ref, row_ref, out_ref, h * HEAD_DIM,
                )

    def w_spec(c):
        return pl.BlockSpec(
            (None, deep, cols), lambda s, w: (c, w[0] * steps + s, first // heads)
        )

    def acc_spec(c):
        return pl.BlockSpec((None, rows, cols), lambda s, w: (c, 0, first // heads))

    in_specs = [pl.BlockSpec((rows, deep), lambda s, w: (0, s)) for _ in parts]
    in_specs += [w_spec(c) for c in range(kinds)] + [acc_spec(c) for c in range(kinds)]
    in_specs += [
        pl.BlockSpec((heads, 2, HEAD_DIM), lambda s, w: (first // heads, 0, 0)),
        pl.BlockSpec((rows, 1), lambda s, w: (0, 0)),
        pl.BlockSpec((1, rows), lambda s, w: (0, 0)),
    ]
    return pl.pallas_call(
        kernel,
        grid_spec=pltpu.PrefetchScalarGridSpec(
            num_scalar_prefetch=1,
            grid=(steps,),
            in_specs=in_specs,
            out_specs=pl.BlockSpec((rows, cols), lambda s, w: (0, 0)),
            scratch_shapes=[pltpu.VMEM((kinds, rows, cols), jnp.float32)],
        ),
        out_shape=jax.ShapeDtypeStruct((rows, cols), jnp.bfloat16),
        compiler_params=pltpu.CompilerParams(vmem_limit_bytes=VMEM),
        cost_estimate=COST,
    )(
        jnp.reshape(which, (1,)), *parts, *([weight] * kinds), *([acc] * kinds),
        gains, block_col, block_row,
    )


def project_out(pieces, weight, which, acc, residual):
    rows = pieces[0][0].shape[0]
    depth = sum(piece[0].shape[1] for piece in pieces)
    width = which[1]
    above = which[3] // depth
    high = pick(rows, 256)
    flat = [array for piece in pieces for array in piece]

    def kernel(which_ref, *refs):
        out_ref = refs[-1]
        w_ref = refs[len(flat)]
        total = None if acc is None else refs[len(flat) + 1][...]
        first = begin = 0
        for piece in pieces:
            x = whole(refs[first : first + len(piece)])
            first += len(piece)
            part = jnp.dot(
                x, w_ref[begin : begin + x.shape[1], :], preferred_element_type=jnp.float32
            )
            begin += x.shape[1]
            total = part if total is None else total + part
        if residual is not None:
            total = refs[-2][...].astype(jnp.float32) + total
        out_ref[...] = total.astype(out_ref.dtype)

    tile = pl.BlockSpec((high, width), lambda i, w: (i, 0))
    in_specs = [pl.BlockSpec((high, p.shape[1]), lambda i, w: (i, 0)) for p in flat]
    in_specs.append(pl.BlockSpec((None, depth, width), lambda i, w: (w[0], above, w[1])))
    args = [jnp.stack([which[0], which[2]]), *flat, weight]
    for extra in (acc, residual):
        if extra is not None:
            in_specs.append(tile)
            args.append(extra)
    out_type = jnp.float32 if residual is None else jnp.bfloat16
    return pl.pallas_call(
        kernel,
        grid_spec=pltpu.PrefetchScalarGridSpec(
            num_scalar_prefetch=1, grid=(rows // high,), in_specs=in_specs, out_specs=tile
        ),
        out_shape=jax.ShapeDtypeStruct((rows, width), out_type),
        compiler_params=pltpu.CompilerParams(vmem_limit_bytes=VMEM),
        cost_estimate=COST,
    )(*args)


def exchange_out_weight(out_weight, n, groups):
    depth, features = out_weight.shape
    place = lax.axis_index("mp")
    piece = depth // groups
    cols = features // n
    mine = lax.dynamic_slice_in_dim(out_weight, lax.axis_index("dp") * piece, piece, axis=0)

    def columns(index):
        return lax.dynamic_slice_in_dim(mine, index * cols, cols, axis=1)

    received = [(place, columns(place))]
    for d in range(1, n):
        sent = lax.ppermute(
            columns((place + d) % n), "mp", [(i, (i + d) % n) for i in range(n)]
        )
        received.append(((place - d) % n, sent))
    return received


def gather_out_weight(received, after):
    arrays = lax.optimization_barrier((*[array for _, array in received], after))[:-1]
    pieces = jnp.zeros((len(arrays), *arrays[0].shape), arrays[0].dtype)
    for (origin, _), array in zip(received, arrays):
        pieces = lax.dynamic_update_slice_in_dim(pieces, array[None], origin, axis=0)
    return lax.all_gather(pieces, "dp", axis=1, tiled=True)


def shards(tokens, dest_pos, src_row, segment_ids, norm_gain, qkv_weight, qk_gain, out_weight):
    groups = lax.axis_size("dp")
    n = lax.axis_size("mp")
    place = lax.axis_index("mp")
    rows, cols = tokens.shape
    features = cols * n
    reach = 3 * rows // (2 * groups)
    heads = qkv_weight.shape[2] // HEAD_DIM

    segment = lax.all_gather(segment_ids, "dp", tiled=True)[dest_pos]
    block = dest_pos // rows * groups + segment
    block_col = block[:, None]
    block_row = block[None, :]
    gains = jnp.transpose(qk_gain, (1, 0, 2))

    with jax.named_scope("normalize"):
        values = tokens.astype(jnp.float32)
        moments = lax.psum((jnp.sum(values, axis=1), jnp.sum(values * values, axis=1)), "mp")
        average = moments[0] / features
        variance = moments[1] / features - average * average
        gain = lax.dynamic_slice_in_dim(norm_gain, place * cols, cols)
        centred = values - average[:, None]
        normed = (centred * lax.rsqrt(variance + EPS)[:, None] * gain).astype(jnp.bfloat16)

    sources = origins("mp", n)

    def step_project(parts, origin, acc):
        with jax.named_scope("project"):
            return project(parts, qkv_weight, origin, acc)

    line = Relay(normed, "mp", n)
    line.step(1)
    projected = step_project([normed], place, None)
    for s in range(2, n):
        line.step(s, projected, block)
        projected = step_project(line.arrived(s - 2), sources[s - 2], projected)
    last = line.arrived(n - 2)
    after = lax.optimization_barrier((out_weight, projected, *last))
    received = exchange_out_weight(after[0], n, groups)

    chunk = 2 if heads % 2 == 0 else 1
    contexts, lines = [], []
    for first in range(0, heads, chunk):
        if contexts:
            gains, _ = lax.optimization_barrier((gains, contexts[-1]))
        with jax.named_scope("attend"):
            context = attend(
                last, qkv_weight, sources[n - 2], projected, gains, block_col, block_row,
                first, chunk, reach,
            )
        contexts.append(context)
        lines.append(Relay(context, "mp", n))
        lines[-1].step(1)
    out_columns = gather_out_weight(received, contexts[min(1, len(contexts) - 1)])

    zero = jnp.zeros((), jnp.int32)

    def step_out(k, acc, residual, first, end):
        pieces = [line.arrived(k) for line in lines[first:end]]
        where = (sources[k], cols, zero, first * chunk * HEAD_DIM)
        return project_out(pieces, out_columns, where, acc, residual)

    total = project_out(
        [[c] for c in contexts], out_weight[None], (zero, cols, place, 0), None, None
    )
    count = len(lines)
    for s in range(2, n):
        for line in lines[:-1]:
            line.step(s)
        lines[-1].step(s, total)
        total = step_out(s - 2, total, None, 0, count)
    total = step_out(n - 2, total, None, 0, count - 1)
    return step_out(n - 2, total, tokens, count - 1, count)


def solution(mesh):
    in_specs = (
        P("dp", "mp"),
        P("dp"),
        P("dp"),
        P("dp"),
        P(),
        P(None, None, "mp"),
        P(None, "mp", None),
        P("mp", None),
    )
    out_specs = P("dp", "mp")
    return jax.shard_map(shards, mesh=mesh, in_specs=in_specs, out_specs=out_specs, check_vma=False)
```

time: 545 us -> 399 us (0.73)
  blocking collectives: 193 us -> 22.7 us
  waiting for transfers between devices: 140 us -> 178 us
  other arithmetic: 21.5 us -> 9.93 us
    psum x1, blocking collectives: 184 us -> 13.6 us  [shards(): lax.psum((jnp.sum(values, axis=1), jnp.sum(values * values, axis=1)), 'mp')]
    ppermute x20, waiting for transfers between devices: 61.6 us -> 162 us  [step(): self.got[s, kind] = lax.ppermute(source, self.axis, self.steps[s, kind])]
    ppermute x3, waiting for transfers between devices: 78 us -> 0.01 us  [exchange_out_weight(): lax.ppermute(columns((place + d) % n), 'mp', [(i, (i + d) % n) for i in r...]
    pallas_call x4 -> x3, Pallas kernels: 64.7 us -> 43.5 us  [project(): pl.pallas_call(kernel, grid_spec=pltpu.PrefetchScalarGridSpec(num_scalar_...]
    pallas_call x3, Pallas kernels: 24.3 us -> 42.6 us  [attend(): pl.pallas_call(kernel, grid_spec=pltpu.PrefetchScalarGridSpec(num_scalar_...]
    all_gather x1, waiting for transfers between devices: 0.01 us -> 15.2 us  [gather_out_weight(): return lax.all_gather(pieces, 'dp', axis=1, tiled=True)]
    convert_element_type x1, other arithmetic: 11.6 us -> 2.66 us  [shards(): (centred * lax.rsqrt(variance + EPS)[:, None] * gain).astype(jnp.bfloat16)]
    select_n x6 -> x0, other arithmetic: 8.9 us -> none  [relay(): value = jnp.where(jnp.asarray(here)[place], got[key], value)]
  transfers between devices with their start and end apart: 24 -> 24, of which waited for: 11 -> 8; matrix products, arithmetic and copies ran while one was open for 7% -> 3% of each run, Pallas kernels for 16% -> 31%
where the time goes in v2:
time: 399 us; the launch traced here: 398 us
  waiting for transfers between devices  178 us (45%)
  Pallas kernels  129 us (32%)
  starting transfers between devices  28.3 us (7%)
  blocking collectives  22.7 us (6%)
  local copies, waits for them, and re-layouts  16 us (4%)
  between operations  13.9 us (3%)
  other arithmetic  9.93 us (2%)
    ppermute x20, waiting for transfers between devices, step(): self.got[s, kind] = lax.ppermute(source, self.axis, self.steps[s, kind])  162 us
    pallas_call x3, Pallas kernels, project(): pl.pallas_call(kernel, grid_spec=pltpu.PrefetchScalarGridSpec(num_scalar_...  43.5 us
    pallas_call x5, Pallas kernels, project_out(): pl.pallas_call(kernel, grid_spec=pltpu.PrefetchScalarGridSpec(num_scalar_...  43.3 us
    pallas_call x3, Pallas kernels, attend(): pl.pallas_call(kernel, grid_spec=pltpu.PrefetchScalarGridSpec(num_scalar_...  42.6 us
    ppermute x20, starting transfers between devices, step(): self.got[s, kind] = lax.ppermute(source, self.axis, self.steps[s, kind])  24.4 us
    all_gather x1, waiting for transfers between devices, gather_out_weight(): return lax.all_gather(pieces, 'dp', axis=1, tiled=True)  15.2 us
    psum x1, blocking collectives, shards(): lax.psum((jnp.sum(values, axis=1), jnp.sum(values * values, axis=1)), 'mp')  13.6 us
    all_gather x1, blocking collectives, shards(): segment = lax.all_gather(segment_ids, 'dp', tiled=True)[dest_pos]  9.07 us
  transfers between devices with their start and end apart: 24, of which 8 were waited for; matrix products, arithmetic and copies ran while one was open for 3% of the time, Pallas kernels for 31%

profile of v2, /device:TPU:0, one launch (start us, length us, event | category | flops | bytes accessed | tf_op | source)
XLA Modules:
  0.0 397.7 jit_solution(7704089217507683189)
XLA Ops:
  6.5 3.1 convert_reduce_fusion
  10.4 13.6 %all-reduce = (f32[1024]{0:T(1024)S(1)}, f32[1024]{0:T(1024)S(1)}) all-reduce(f32[1024]{0:T(1024)S(1)} %get-tuple-element.56, f32[1024]{0:T(1024)S(1)} %get-tuple-element.55), channel_id=1, replica_groups=mesh['dp'=8,'mp'=4] {'mp'}, use_global_device_ids=true, to_apply=%region_3.4 | all-reduce | flops 2048 | bytes 16384 | tf_op jit(solution)/shard_map/normalize/psum | solution.py:313
  24.1 2.7 fusion.2.refs_0_
  26.7 0.9 collective-permute-start
  27.6 1.2 collective-permute-start.1
  28.7 9.1 %all_gather.6 = s32[8192]{0:T(1024)S(1)} all-gather(s32[1024]{0:T(1024)S(1)} %copy-done.19), channel_id=1, replica_groups=mesh['dp'=8,'mp'=4] {'dp'}, dimensions={0}, use_global_device_ids=true | all-gather | bytes 36864 | tf_op jit(solution)/shard_map/all_gather | solution.py:305
  37.8 6.1 %gather_fusion = s32[1024]{0:T(1024)S(1)} fusion(s32[8192]{0:T(1024)S(1)} %all_gather.6, s32[1024]{0:T(1024)S(1)} %fusion.7), kind=kCustom, calls=%fused_computation | custom fusion | bytes 12288 | tf_op jit(solution)/shard_map/gather | solution.py:305
  44.0 12.3 %project.3.refs_2_ = f32[3,1024,768]{2,1,0:T(8,128)} custom-call(s32[1]{0:T(128)} %bitcast.1.which_ref, bf16[1024,1536]{1,0:T(8,128)(2,1)} %fusion.2.refs_0_, bf16[3,6144,768]{2,1,0:T(8,128)(2,1)} %refs_4_.6), custom_call_target="tpu_custom_call" | custom-call | flops 7247757312 | bytes 25952256 | tf_op jit(solution)/shard_map/project/pallas_call | solution.py:104
  56.3 1.7 copy-done.3
  58.0 37.7 %collective-permute-done.1.refs_0_ = bf16[1024,1536]{1,0:T(8,128)(2,1)} collective-permute-done((bf16[1024,1536]{1,0:T(8,128)(2,1)}, bf16[1024,1536]{1,0:T(8,128)(2,1)}, u32[]{:S(2)}, u32[]{:S(2)}) %collective-permute-start.1) | collective-permute-done | bytes 3145760 | tf_op jit(solution)/shard_map/ppermute | solution.py:54
  95.7 0.9 collective-permute-start.2
  97.2 1.3 collective-permute-start.4
  98.5 15.2 %project.4.refs_3_ = f32[3,1024,768]{2,1,0:T(8,128)} custom-call(s32[1]{0:T(128)} %bitcast.2.which_ref, bf16[1024,1536]{1,0:T(8,128)(2,1)} %collective-permute-done.1.refs_0_, bf16[3,6144,768]{2,1,0:T(8,128)(2,1)} %refs_4_.6, f32[3,1024,768]{2,1,0:T(8,128)} %project.3.refs_2_), custom_call_target="tpu_custom_call", output_to_operand_aliasing={{}: (3, {})} | custom-call | flops 7247757312 | bytes 25952256 | tf_op jit(solution)/shard_map/project/pallas_call | solution.py:104
  113.7 1.3 collective-permute-start.3
  115.0 55.2 %collective-permute-done.4.refs_1_ = bf16[1024,1536]{1,0:T(8,128)(2,1)} collective-permute-done((bf16[1024,1536]{1,0:T(8,128)(2,1)}, bf16[1024,1536]{1,0:T(8,128)(2,1)}, u32[]{:S(2)}, u32[]{:S(2)}) %collective-permute-start.4) | collective-permute-done | bytes 3145760 | tf_op jit(solution)/shard_map/ppermute | solution.py:54
  170.3 16.0 %project.5.refs_5_.refs_6_.refs_7_ = f32[3,1024,768]{2,1,0:T(8,128)} custom-call(s32[1]{0:T(128)} %bitcast.3.which_ref, bf16[1024,1536]{1,0:T(8,128)(2,1)} %copy-done.3, bf16[1024,1536]{1,0:T(8,128)(2,1)} %collective-permute-done.4.refs_1_, bf16[3,6144,768]{2,1,0:T(8,128)(2,1)} %refs_4_.6, ...), custom_call_target="tpu_custom_call", output_to_operand_aliasing={{}: (4, {})} | custom-call | flops 7247757312 | bytes 25952256 | tf_op jit(solution)/shard_map/project/pallas_call | solution.py:104
  186.3 48.7 %collective-permute-done.3.refs_1_ = bf16[1024,1536]{1,0:T(8,128)(2,1)} collective-permute-done((bf16[1024,1536]{1,0:T(8,128)(2,1)S(1)}, bf16[1024,1536]{1,0:T(8,128)(2,1)}, u32[]{:S(2)}, u32[]{:S(2)}) %collective-permute-start.3) | collective-permute-done | bytes 3145760 | tf_op jit(solution)/shard_map/ppermute | solution.py:54
  235.0 2.0 fusion.9
  237.1 2.3 collective-permute-start.11
  239.3 1.5 collective-permute-start.12
  240.9 1.0 copy.14.refs_9_
  241.9 14.0 %attend.3.refs_0_ = bf16[1024,256]{1,0:T(8,128)(2,1)} custom-call(s32[1]{0:T(128)} %bitcast.which_ref, bf16[1024,1536]{1,0:T(8,128)(2,1)} %copy-done.1, bf16[1024,1536]{1,0:T(8,128)(2,1)} %collective-permute-done.3.refs_1_, bf16[3,6144,768]{2,1,0:T(8,128)(2,1)} %refs_4_.6, bf16[3,6144,768]{2,1,0:T(8,128)(2,1)} %refs_4_.6, bf16[3,6144,768]{2,1,0:T(8,128)(2,1)} %refs_4_.6, ...), custom_call_target="tpu_custom_call" | custom-call | flops 1024 | bytes 1024 | tf_op jit(solution)/shard_map/attend/pallas_call | solution.py:206
  255.9 13.9 %attend.4.refs_1_ = bf16[1024,256]{1,0:T(8,128)(2,1)} custom-call(s32[1]{0:T(128)} %bitcast.which_ref, bf16[1024,1536]{1,0:T(8,128)(2,1)} %copy-done.1, bf16[1024,1536]{1,0:T(8,128)(2,1)} %collective-permute-done.3.refs_1_, bf16[3,6144,768]{2,1,0:T(8,128)(2,1)} %refs_4_.6, bf16[3,6144,768]{2,1,0:T(8,128)(2,1)} %refs_4_.6, bf16[3,6144,768]{2,1,0:T(8,128)(2,1)} %refs_4_.6, ...), custom_call_target="tpu_custom_call" | custom-call | flops 1024 | bytes 1024 | tf_op jit(solution)/shard_map/attend/pallas_call | solution.py:206
  270.1 1.0 copy-done.2
  271.8 3.9 collective-permute-start.9
  276.4 1.3 collective-permute-start.8
  277.7 14.7 %attend.5.refs_2_ = bf16[1024,256]{1,0:T(8,128)(2,1)} custom-call(s32[1]{0:T(128)} %bitcast.which_ref, bf16[1024,1536]{1,0:T(8,128)(2,1)} %copy-done.1, bf16[1024,1536]{1,0:T(8,128)(2,1)} %collective-permute-done.3.refs_1_, bf16[3,6144,768]{2,1,0:T(8,128)(2,1)} %refs_4_.6, bf16[3,6144,768]{2,1,0:T(8,128)(2,1)} %refs_4_.6, bf16[3,6144,768]{2,1,0:T(8,128)(2,1)} %refs_4_.6, ...), custom_call_target="tpu_custom_call" | custom-call | flops 1024 | bytes 1024 | tf_op jit(solution)/shard_map/attend/pallas_call | solution.py:206
  292.4 1.1 collective-permute-start.6
  294.8 7.9 %shard_map.82.refs_4_ = f32[1024,1536]{1,0:T(8,128)} custom-call(s32[2]{0:T(128)} %pad_add_fusion.3.which_ref, bf16[1024,256]{1,0:T(8,128)(2,1)} %attend.3.refs_0_, bf16[1024,256]{1,0:T(8,128)(2,1)} %attend.4.refs_1_, bf16[1024,256]{1,0:T(8,128)(2,1)} %attend.5.refs_2_, bf16[1,768,6144]{2,1,0:T(8,128)(2,1)} %bitcast.16), custom_call_target="tpu_custom_call" | custom-call | flops 1024 | bytes 1024 | tf_op jit(solution)/shard_map/pallas_call | solution.py:258
  302.7 1.5 collective-permute-start.18
  304.9 1.8 collective-permute-done.6.refs_2_
  307.4 1.3 collective-permute-start.21
  308.7 1.2 pad_add_fusion.1.which_ref
  309.9 1.3 collective-permute-start.20
  311.2 1.3 collective-permute-start.22
  313.3 1.3 collective-permute-start.19
  314.6 15.2 %all-gather.2.cloned.1.call-done.refs_3_.refs_6_.refs_4_.refs_2_ = bf16[4,768,1536]{2,1,0:T(8,128)(2,1)} async-done(((bf16[4,96,1536]{2,1,0:T(8,128)(2,1)}), bf16[4,768,1536]{2,1,0:T(8,128)(2,1)}) %all-gather.2.cloned.1.call-update) | async-done | bytes 9437200 | tf_op jit(solution)/shard_map/all_gather | solution.py:293
  329.8 9.5 %shard_map.83.refs_7_ = f32[1024,1536]{1,0:T(8,128)} custom-call(s32[2]{0:T(128)} %pad_add_fusion.1.which_ref, bf16[1024,256]{1,0:T(8,128)(2,1)} %copy-done.11, bf16[1024,256]{1,0:T(8,128)(2,1)} %copy-done.9, bf16[1024,256]{1,0:T(8,128)(2,1)} %collective-permute-done.6.refs_2_, ...), custom_call_target="tpu_custom_call" | custom-call | flops 1024 | bytes 1024 | tf_op jit(solution)/shard_map/pallas_call | solution.py:258
  339.3 1.3 collective-permute-start.16
  340.7 1.3 collective-permute-start.13
  342.0 1.2 pad_add_fusion.which_ref
  343.2 1.2 pad_add_fusion.2.which_ref
  344.4 7.4 %collective-permute-done.22.refs_5_ = bf16[1024,256]{1,0:T(8,128)(2,1)} collective-permute-done((bf16[1024,256]{1,0:T(8,128)(2,1)S(1)}, bf16[1024,256]{1,0:T(8,128)(2,1)}, u32[]{:S(2)}, u32[]{:S(2)}) %collective-permute-start.22) | collective-permute-done | bytes 524320 | tf_op jit(solution)/shard_map/ppermute | solution.py:54
  351.8 9.7 %shard_map.84.refs_5_ = f32[1024,1536]{1,0:T(8,128)} custom-call(s32[2]{0:T(128)} %pad_add_fusion.which_ref, bf16[1024,256]{1,0:T(8,128)(2,1)} %copy-done.7, bf16[1024,256]{1,0:T(8,128)(2,1)} %collective-permute-done.20.refs_1_, bf16[1024,256]{1,0:T(8,128)(2,1)} %copy-done.6, bf16[1024,256]{1,0:T(8,128)(2,1)} %copy-done.12, bf16[1024,256]{1,0:T(8,128)(2,1)} %copy-done.8, ...), custom_call_target="tpu_custom_call" | custom-call | flops 1024 | bytes 1024 | tf_op jit(solution)/shard_map/pallas_call | solution.py:258
  361.6 1.5 collective-permute-done.19.refs_3_
  363.1 10.0 %collective-permute-done.16.refs_1_ = bf16[1024,256]{1,0:T(8,128)(2,1)S(1)} collective-permute-done((bf16[1024,256]{1,0:T(8,128)(2,1)S(1)}, bf16[1024,256]{1,0:T(8,128)(2,1)S(1)}, u32[]{:S(2)}, u32[]{:S(2)}) %collective-permute-start.16) | collective-permute-done | bytes 524320 | tf_op jit(solution)/shard_map/ppermute | solution.py:54
  373.9 8.7 %shard_map.85.refs_3_ = f32[1024,1536]{1,0:T(8,128)} custom-call(s32[2]{0:T(128)} %pad_add_fusion.2.which_ref, bf16[1024,256]{1,0:T(8,128)(2,1)} %copy-done.14, bf16[1024,256]{1,0:T(8,128)(2,1)} %copy-done.16, bf16[1024,256]{1,0:T(8,128)(2,1)} %collective-permute-done.18.refs_2_, bf16[1024,256]{1,0:T(8,128)(2,1)} %collective-permute-done.19.refs_3_, ...), custom_call_target="tpu_custom_call" | custom-call | flops 1024 | bytes 1024 | tf_op jit(solution)/shard_map/pallas_call | solution.py:258
  383.4 7.4 %shard_map.86 = bf16[1024,1536]{1,0:T(8,128)(2,1)} custom-call(s32[2]{0:T(128)} %pad_add_fusion.2.which_ref, bf16[1024,256]{1,0:T(8,128)(2,1)} %copy-done.10, bf16[1024,256]{1,0:T(8,128)(2,1)} %copy-done.13, bf16[4,768,1536]{2,1,0:T(8,128)(2,1)} %all-gather.2.cloned.1.call-done.refs_3_.refs_6_.refs_4_.refs_2_, f32[1024,1536]{1,0:T(8,128)} %shard_map.85.refs_3_, ...), custom_call_target="tpu_custom_call" | custom-call | flops 1024 | bytes 1024 | tf_op jit(solution)/shard_map/pallas_call | solution.py:258
  (75 shorter events, 8.3 us)
Async XLA Ops:
  6.5 17.5 %copy-start = (bf16[1024,1536]{1,0:T(8,128)(2,1)S(1)}, bf16[1024,1536]{1,0:T(8,128)(2,1)}, u32[]{:S(2)}) copy-start(bf16[1024,1536]{1,0:T(8,128)(2,1)} %refs_4_.7) | copy-start | bytes 9437188
  6.5 323.3 %all-gather.2.cloned.1.call-start = ((), (), s32[]{:S(2)}) async-start(), calls=%async_computation | async-start | bytes 10616832 | tf_op jit(solution)/shard_map/all_gather | solution.py:293
  24.0 4.7 %copy-start.19 = (s32[1024]{0:T(1024)S(1)}, s32[1024]{0:T(1024)}, u32[]{:S(2)}) copy-start(s32[1024]{0:T(1024)} %param.11) | copy-start | bytes 12292
  24.0 13.8 %copy-start.18 = (s32[1024]{0:T(1024)S(1)}, s32[1024]{0:T(1024)}, u32[]{:S(2)}) copy-start(s32[1024]{0:T(1024)} %param.10) | copy-start | bytes 12292
  26.7 29.6 %collective-permute-start = (bf16[1024,1536]{1,0:T(8,128)(2,1)}, bf16[1024,1536]{1,0:T(8,128)(2,1)S(1)}, u32[]{:S(2)}, u32[]{:S(2)}) collective-permute-start(bf16[1024,1536]{1,0:T(8,128)(2,1)} %fusion.2.refs_0_), channel_id=1, source_target_pairs={{1,2},{2,1},{5,6},{6,5},{9,10},{10,9},{13,14},{14,13},{17,18},{18,... | collective-permute-start | bytes 9437192 | tf_op jit(solution)/shard_map/ppermute | solution.py:54
  27.6 68.1 %collective-permute-start.1 = (bf16[1024,1536]{1,0:T(8,128)(2,1)}, bf16[1024,1536]{1,0:T(8,128)(2,1)}, u32[]{:S(2)}, u32[]{:S(2)}) collective-permute-start(bf16[1024,1536]{1,0:T(8,128)(2,1)} %fusion.2.refs_0_), channel_id=1, source_target_pairs={{0,1},{1,0},{2,3},{3,2},{4,5},{5,4},{6,7},{7,6},{8,9},{9,8},{10,11... | collective-permute-start | bytes 9437192 | tf_op jit(solution)/shard_map/ppermute | solution.py:54
  44.0 196.9 %copy-start.17 = (s32[1024]{0:T(1024)}, s32[1024]{0:T(1024)S(1)}, u32[]{:S(2)}) copy-start(s32[1024]{0:T(1024)S(1)} %fusion.6) | copy-start | bytes 12292
  44.0 52.6 %copy-start.20 = (s32[4,3]{1,0:T(4,128)S(1)}, s32[4,3]{1,0:T(4,128)}, u32[]{:S(2)}) copy-start(s32[4,3]{1,0:T(4,128)} %constant.136.clone) | copy-start | bytes 148
  56.3 1.7 copy-start.3
  95.7 18.0 %collective-permute-start.2 = (bf16[1024,1536]{1,0:T(8,128)(2,1)}, bf16[1024,1536]{1,0:T(8,128)(2,1)S(1)}, u32[]{:S(2)}, u32[]{:S(2)}) collective-permute-start(bf16[1024,1536]{1,0:T(8,128)(2,1)} %collective-permute-done.1.refs_0_), channel_id=1, source_target_pairs={{1,2},{2,1},{5,6},{6,5},{9,10},{10,9},{13,14},{14,13},{17,18},{18,... | collective-permute-start | bytes 9437192 | tf_op jit(solution)/shard_map/ppermute | solution.py:54
  97.2 73.0 %collective-permute-start.4 = (bf16[1024,1536]{1,0:T(8,128)(2,1)}, bf16[1024,1536]{1,0:T(8,128)(2,1)}, u32[]{:S(2)}, u32[]{:S(2)}) collective-permute-start(bf16[1024,1536]{1,0:T(8,128)(2,1)} %copy-done.3), channel_id=1, source_target_pairs={{1,0},{2,3},{5,4},{6,7},{9,8},{10,11},{13,12},{14,15},{17,16},{18,... | collective-permute-start | bytes 9437192 | tf_op jit(solution)/shard_map/ppermute | solution.py:54
  113.7 72.6 %copy-start.1 = (bf16[1024,1536]{1,0:T(8,128)(2,1)}, bf16[1024,1536]{1,0:T(8,128)(2,1)S(1)}, u32[]{:S(2)}) copy-start(bf16[1024,1536]{1,0:T(8,128)(2,1)S(1)} %collective-permute-done.2.refs_0_) | copy-start | bytes 9437188
  113.7 121.3 %collective-permute-start.3 = (bf16[1024,1536]{1,0:T(8,128)(2,1)S(1)}, bf16[1024,1536]{1,0:T(8,128)(2,1)}, u32[]{:S(2)}, u32[]{:S(2)}) collective-permute-start(bf16[1024,1536]{1,0:T(8,128)(2,1)S(1)} %collective-permute-done.2.refs_0_), channel_id=1, source_target_pairs={{1,0},{2,3},{5,4},{6,7},{9,8},{10,11},{13,12},{14,15},{17,16},{18,... | collective-permute-start | bytes 9437192 | tf_op jit(solution)/shard_map/ppermute | solution.py:54
  237.0 32.8 %collective-permute-start.10 = (bf16[96,1536]{1,0:T(8,128)(2,1)S(1)}, bf16[96,1536]{1,0:T(8,128)(2,1)S(1)}, u32[]{:S(2)}, u32[]{:S(2)}) collective-permute-start(bf16[96,1536]{1,0:T(8,128)(2,1)S(1)} %get-tuple-element.61), channel_id=1, source_target_pairs={{0,1},{1,2},{2,3},{3,0},{4,5},{5,6},{6,7},{7,4},{8,9},{9,10},{10,1... | collective-permute-start | bytes 884744 | tf_op jit(solution)/shard_map/ppermute | solution.py:281
  237.1 32.8 %collective-permute-start.11 = (bf16[96,1536]{1,0:T(8,128)(2,1)S(1)}, bf16[96,1536]{1,0:T(8,128)(2,1)S(1)}, u32[]{:S(2)}, u32[]{:S(2)}) collective-permute-start(bf16[96,1536]{1,0:T(8,128)(2,1)S(1)} %get-tuple-element.60), channel_id=1, source_target_pairs={{0,2},{1,3},{2,0},{3,1},{4,6},{5,7},{6,4},{7,5},{8,10},{9,11},{10,... | collective-permute-start | bytes 884744 | tf_op jit(solution)/shard_map/ppermute | solution.py:281
  239.3 30.5 %collective-permute-start.12 = (bf16[96,1536]{1,0:T(8,128)(2,1)S(1)}, bf16[96,1536]{1,0:T(8,128)(2,1)S(1)}, u32[]{:S(2)}, u32[]{:S(2)}) collective-permute-start(bf16[96,1536]{1,0:T(8,128)(2,1)S(1)} %get-tuple-element.59), channel_id=1, source_target_pairs={{0,3},{1,0},{2,1},{3,2},{4,7},{5,4},{6,5},{7,6},{8,11},{9,8},{10,9... | collective-permute-start | bytes 884744 | tf_op jit(solution)/shard_map/ppermute | solution.py:281
  269.8 1.3 copy-start.5
  269.8 5.9 %copy-start.4 = (bf16[1024,256]{1,0:T(8,128)(2,1)S(1)}, bf16[1024,256]{1,0:T(8,128)(2,1)}, u32[]{:S(2)}) copy-start(bf16[1024,256]{1,0:T(8,128)(2,1)} %attend.3.refs_0_) | copy-start | bytes 1572868
  270.1 1.0 copy-start.2
  271.1 22.4 %collective-permute-start.17 = (bf16[1024,256]{1,0:T(8,128)(2,1)S(1)}, bf16[1024,256]{1,0:T(8,128)(2,1)S(1)}, u32[]{:S(2)}, u32[]{:S(2)}) collective-permute-start(bf16[1024,256]{1,0:T(8,128)(2,1)S(1)} %copy-done.5), channel_id=1, source_target_pairs={{1,2},{2,1},{5,6},{6,5},{9,10},{10,9},{13,14},{14,13},{17,18},{18,... | collective-permute-start | bytes 1572872 | tf_op jit(solution)/shard_map/ppermute | solution.py:54
  271.8 30.9 %collective-permute-start.9 = (bf16[1024,256]{1,0:T(8,128)(2,1)S(1)}, bf16[1024,256]{1,0:T(8,128)(2,1)S(1)}, u32[]{:S(2)}, u32[]{:S(2)}) collective-permute-start(bf16[1024,256]{1,0:T(8,128)(2,1)S(1)} %copy-done.5), channel_id=1, source_target_pairs={{0,1},{1,0},{2,3},{3,2},{4,5},{5,4},{6,7},{7,6},{8,9},{9,8},{10,11... | collective-permute-start | bytes 1572872 | tf_op jit(solution)/shard_map/ppermute | solution.py:54
  275.7 28.5 %collective-permute-start.14 = (bf16[1024,256]{1,0:T(8,128)(2,1)S(1)}, bf16[1024,256]{1,0:T(8,128)(2,1)S(1)}, u32[]{:S(2)}, u32[]{:S(2)}) collective-permute-start(bf16[1024,256]{1,0:T(8,128)(2,1)S(1)} %copy-done.4), channel_id=1, source_target_pairs={{1,2},{2,1},{5,6},{6,5},{9,10},{10,9},{13,14},{14,13},{17,18},{18,... | collective-permute-start | bytes 1572872 | tf_op jit(solution)/shard_map/ppermute | solution.py:54
  276.4 27.8 %collective-permute-start.8 = (bf16[1024,256]{1,0:T(8,128)(2,1)S(1)}, bf16[1024,256]{1,0:T(8,128)(2,1)S(1)}, u32[]{:S(2)}, u32[]{:S(2)}) collective-permute-start(bf16[1024,256]{1,0:T(8,128)(2,1)S(1)} %copy-done.4), channel_id=1, source_target_pairs={{0,1},{1,0},{2,3},{3,2},{4,5},{5,4},{6,7},{7,6},{8,9},{9,8},{10,11... | collective-permute-start | bytes 1572872 | tf_op jit(solution)/shard_map/ppermute | solution.py:54
  292.4 14.3 %collective-permute-start.6 = (bf16[1024,256]{1,0:T(8,128)(2,1)}, bf16[1024,256]{1,0:T(8,128)(2,1)}, u32[]{:S(2)}, u32[]{:S(2)}) collective-permute-start(bf16[1024,256]{1,0:T(8,128)(2,1)} %attend.5.refs_2_), channel_id=1, source_target_pairs={{0,1},{1,0},{2,3},{3,2},{4,5},{5,4},{6,7},{7,6},{8,9},{9,8},{10,11... | collective-permute-start | bytes 1572872 | tf_op jit(solution)/shard_map/ppermute | solution.py:54
  293.6 13.9 %copy-start.6 = (bf16[1024,256]{1,0:T(8,128)(2,1)}, bf16[1024,256]{1,0:T(8,128)(2,1)S(1)}, u32[]{:S(2)}) copy-start(bf16[1024,256]{1,0:T(8,128)(2,1)S(1)} %collective-permute-done.17.refs_2_) | copy-start | bytes 1572868
  293.6 13.2 %collective-permute-start.5 = (bf16[1024,256]{1,0:T(8,128)(2,1)}, bf16[1024,256]{1,0:T(8,128)(2,1)S(1)}, u32[]{:S(2)}, u32[]{:S(2)}) collective-permute-start(bf16[1024,256]{1,0:T(8,128)(2,1)} %attend.5.refs_2_), channel_id=1, source_target_pairs={{1,2},{2,1},{5,6},{6,5},{9,10},{10,9},{13,14},{14,13},{17,18},{18,... | collective-permute-start | bytes 1572872 | tf_op jit(solution)/shard_map/ppermute | solution.py:54
  302.7 27.1 %copy-start.9 = (bf16[1024,256]{1,0:T(8,128)(2,1)}, bf16[1024,256]{1,0:T(8,128)(2,1)S(1)}, u32[]{:S(2)}) copy-start(bf16[1024,256]{1,0:T(8,128)(2,1)S(1)} %collective-permute-done.9.refs_1_) | copy-start | bytes 1572868
  302.7 8.5 %collective-permute-start.18 = (bf16[1024,256]{1,0:T(8,128)(2,1)S(1)}, bf16[1024,256]{1,0:T(8,128)(2,1)}, u32[]{:S(2)}, u32[]{:S(2)}) collective-permute-start(bf16[1024,256]{1,0:T(8,128)(2,1)S(1)} %collective-permute-done.9.refs_1_), channel_id=1, source_target_pairs={{1,2},{2,1},{5,6},{6,5},{9,10},{10,9},{13,14},{14,13},{17,18},{18,... | collective-permute-start | bytes 1572872 | tf_op jit(solution)/shard_map/ppermute | solution.py:54
  304.2 35.1 %copy-start.7 = (bf16[1024,256]{1,0:T(8,128)(2,1)}, bf16[1024,256]{1,0:T(8,128)(2,1)S(1)}, u32[]{:S(2)}) copy-start(bf16[1024,256]{1,0:T(8,128)(2,1)S(1)} %collective-permute-done.14.refs_0_) | copy-start | bytes 1572868
  304.2 7.0 %copy-start.11 = (bf16[1024,256]{1,0:T(8,128)(2,1)}, bf16[1024,256]{1,0:T(8,128)(2,1)S(1)}, u32[]{:S(2)}) copy-start(bf16[1024,256]{1,0:T(8,128)(2,1)S(1)} %collective-permute-done.8.refs_0_) | copy-start | bytes 1572868
  304.2 8.3 %collective-permute-start.15 = (bf16[1024,256]{1,0:T(8,128)(2,1)S(1)}, bf16[1024,256]{1,0:T(8,128)(2,1)S(1)}, u32[]{:S(2)}, u32[]{:S(2)}) collective-permute-start(bf16[1024,256]{1,0:T(8,128)(2,1)S(1)} %collective-permute-done.8.refs_0_), channel_id=1, source_target_pairs={{1,2},{2,1},{5,6},{6,5},{9,10},{10,9},{13,14},{14,13},{17,18},{18,... | collective-permute-start | bytes 1572872 | tf_op jit(solution)/shard_map/ppermute | solution.py:54
  306.7 32.6 %copy-start.8 = (bf16[1024,256]{1,0:T(8,128)(2,1)}, bf16[1024,256]{1,0:T(8,128)(2,1)S(1)}, u32[]{:S(2)}) copy-start(bf16[1024,256]{1,0:T(8,128)(2,1)S(1)} %collective-permute-done.5.refs_4_) | copy-start | bytes 1572868
  306.7 32.6 %collective-permute-start.7 = (bf16[1024,256]{1,0:T(8,128)(2,1)}, bf16[1024,256]{1,0:T(8,128)(2,1)S(1)}, u32[]{:S(2)}, u32[]{:S(2)}) collective-permute-start(bf16[1024,256]{1,0:T(8,128)(2,1)} %collective-permute-done.6.refs_2_), channel_id=1, source_target_pairs={{1,2},{2,1},{5,6},{6,5},{9,10},{10,9},{13,14},{14,13},{17,18},{18,... | collective-permute-start | bytes 1572872 | tf_op jit(solution)/shard_map/ppermute | solution.py:54
  307.4 33.2 %collective-permute-start.21 = (bf16[1024,256]{1,0:T(8,128)(2,1)S(1)}, bf16[1024,256]{1,0:T(8,128)(2,1)S(1)}, u32[]{:S(2)}, u32[]{:S(2)}) collective-permute-start(bf16[1024,256]{1,0:T(8,128)(2,1)S(1)} %collective-permute-done.17.refs_2_), channel_id=1, source_target_pairs={{1,0},{2,3},{5,4},{6,7},{9,8},{10,11},{13,12},{14,15},{17,16},{18,... | collective-permute-start | bytes 1572872 | tf_op jit(solution)/shard_map/ppermute | solution.py:54
  309.9 34.5 %collective-permute-start.20 = (bf16[1024,256]{1,0:T(8,128)(2,1)S(1)}, bf16[1024,256]{1,0:T(8,128)(2,1)}, u32[]{:S(2)}, u32[]{:S(2)}) collective-permute-start(bf16[1024,256]{1,0:T(8,128)(2,1)S(1)} %collective-permute-done.14.refs_0_), channel_id=1, source_target_pairs={{1,0},{2,3},{5,4},{6,7},{9,8},{10,11},{13,12},{14,15},{17,16},{18,... | collective-permute-start | bytes 1572872 | tf_op jit(solution)/shard_map/ppermute | solution.py:54
  311.2 40.6 %collective-permute-start.22 = (bf16[1024,256]{1,0:T(8,128)(2,1)S(1)}, bf16[1024,256]{1,0:T(8,128)(2,1)}, u32[]{:S(2)}, u32[]{:S(2)}) collective-permute-start(bf16[1024,256]{1,0:T(8,128)(2,1)S(1)} %collective-permute-done.5.refs_4_), channel_id=1, source_target_pairs={{1,0},{2,3},{5,4},{6,7},{9,8},{10,11},{13,12},{14,15},{17,16},{18,... | collective-permute-start | bytes 1572872 | tf_op jit(solution)/shard_map/ppermute | solution.py:54
  312.5 0.8 copy-start.14
  313.3 49.7 %collective-permute-start.19 = (bf16[1024,256]{1,0:T(8,128)(2,1)}, bf16[1024,256]{1,0:T(8,128)(2,1)}, u32[]{:S(2)}, u32[]{:S(2)}) collective-permute-start(bf16[1024,256]{1,0:T(8,128)(2,1)} %collective-permute-done.18.refs_2_), channel_id=1, source_target_pairs={{1,0},{2,3},{5,4},{6,7},{9,8},{10,11},{13,12},{14,15},{17,16},{18,... | collective-permute-start | bytes 1572872 | tf_op jit(solution)/shard_map/ppermute | solution.py:54
  329.8 9.5 %copy-start.15 = (bf16[1024,256]{1,0:T(8,128)(2,1)S(1)}, bf16[1024,256]{1,0:T(8,128)(2,1)}, u32[]{:S(2)}) copy-start(bf16[1024,256]{1,0:T(8,128)(2,1)} %copy-done.14) | copy-start | bytes 1572868
  339.3 22.2 %copy-start.10 = (bf16[1024,256]{1,0:T(8,128)(2,1)}, bf16[1024,256]{1,0:T(8,128)(2,1)S(1)}, u32[]{:S(2)}) copy-start(bf16[1024,256]{1,0:T(8,128)(2,1)S(1)} %collective-permute-done.7.refs_0_) | copy-start | bytes 1572868
  339.3 33.7 %collective-permute-start.16 = (bf16[1024,256]{1,0:T(8,128)(2,1)S(1)}, bf16[1024,256]{1,0:T(8,128)(2,1)S(1)}, u32[]{:S(2)}, u32[]{:S(2)}) collective-permute-start(bf16[1024,256]{1,0:T(8,128)(2,1)S(1)} %copy-done.15), channel_id=1, source_target_pairs={{1,0},{2,3},{5,4},{6,7},{9,8},{10,11},{13,12},{14,15},{17,16},{18,... | collective-permute-start | bytes 1572872 | tf_op jit(solution)/shard_map/ppermute | solution.py:54
  340.7 11.2 %copy-start.12 = (bf16[1024,256]{1,0:T(8,128)(2,1)}, bf16[1024,256]{1,0:T(8,128)(2,1)S(1)}, u32[]{:S(2)}) copy-start(bf16[1024,256]{1,0:T(8,128)(2,1)S(1)} %collective-permute-done.21.refs_3_) | copy-start | bytes 1572868
  340.7 41.9 %collective-permute-start.13 = (bf16[1024,256]{1,0:T(8,128)(2,1)S(1)}, bf16[1024,256]{1,0:T(8,128)(2,1)S(1)}, u32[]{:S(2)}, u32[]{:S(2)}) collective-permute-start(bf16[1024,256]{1,0:T(8,128)(2,1)S(1)} %collective-permute-done.7.refs_0_), channel_id=1, source_target_pairs={{1,0},{2,3},{5,4},{6,7},{9,8},{10,11},{13,12},{14,15},{17,16},{18,... | collective-permute-start | bytes 1572872 | tf_op jit(solution)/shard_map/ppermute | solution.py:54
  373.1 0.8 copy-start.16
  382.6 0.8 copy-start.13
Sparse Core Ops, SparseCore 0:
  271.3 58.4 all-gather.1
